TPU v7x, 32 devices: a whole 2x2x4 slice. The times are simulated.
32 devices in a mesh: dp: 8 (over z, y), expert: 4 (over x, core).
Axes of the slice: x: 2, y: 2, z: 4, core: 2. Of those that a mesh axis runs over, the one named last changes fastest.
Arguments:
- tokens: bfloat16 [8192, 768], P(('expert', 'dp')), may hold values from -6 to 6
- lengths: int32 [8], replicated, may hold values from 256 to 1024, as said below
- expert_ids: int32 [8192, 1], P(('expert', 'dp')), may hold values from 0 to 7; in each aligned block of 256 rows (0 to 255, 256 to 511, ...) at most 48 rows name the same one
- gain_one: bfloat16 [768], replicated, may hold values from 0.5 to 1.5
- w_query: bfloat16 [768, 768], replicated, may hold values from -0.02734375 to 0.02734375
- w_key: bfloat16 [768, 768], replicated, may hold values from -0.21875 to 0.21875
- w_value: bfloat16 [768, 768], replicated, may hold values from -0.21875 to 0.21875
- w_output: bfloat16 [768, 768], replicated, may hold values from -2.5 to 2.5
- bias_table: bfloat16 [32, 12], replicated, may hold values from -4 to 4
- gain_two: bfloat16 [768], replicated, may hold values from 0.5 to 1.5
- w_router: bfloat16 [768, 8], replicated, may hold values from -0.15625 to 0.15625
- w_in: bfloat16 [8, 768, 3072], P('expert'), may hold values from -0.21875 to 0.21875
- w_out: bfloat16 [8, 3072, 768], P('expert'), may hold values from -1.75 to 1.75
- cotangent: bfloat16 [8192, 768], P(('expert', 'dp')), may hold values from -6 to 6
Outputs:
- output: bfloat16 [8192, 768], P(('expert', 'dp'))
- d_tokens: float32 [8192, 768], P(('expert', 'dp'))
- d_gain_one: float32 [768], replicated
- d_query: float32 [768, 768], replicated
- d_key: float32 [768, 768], replicated
- d_value: float32 [768, 768], replicated
- d_output: float32 [768, 768], replicated
- d_table: float32 [32, 12], replicated
- d_gain_two: float32 [768], replicated
- d_router: float32 [768, 8], replicated
- d_in: float32 [8, 768, 3072], P('expert', 'dp')
- d_out: float32 [8, 3072, 768], P('expert', 'dp')
Inputs may be any that keep to these rules, and one draw needn't show every extreme that they name: `lengths`: one sequence of every 2 consecutive ones has length 1024. `expert_ids`: in the rows of one device (aligned blocks of 256 rows) no expert is chosen more than 48 times.
All inputs are finite; a program needn't handle non-finite values.
Results may differ from a plain program's by a relative error of at most 0.015.
Values may be sent and summed in bfloat16 or wider, within the bound.
A program may use at most 512 MiB of HBM per device.

v0:
```python
import math

import jax
import jax.numpy as jnp
from jax import lax
from jax.sharding import PartitionSpec as P

BUCKETS = 32
EXACT = 8


def partner(array, axis, apart):
    return lax.ppermute(array, axis, [(i, i ^ 1 << apart) for i in range(lax.axis_size(axis))])


def carried_in(value, axis, join, neutral):
    count, mine = (lax.axis_size(axis), lax.axis_index(axis))
    pieces = lax.all_gather(value, axis)
    subtotal = jnp.full_like(value, 0) + jnp.asarray(neutral, value.dtype)

    def hop(position, subtotal):
        longer = join(subtotal, pieces[position])
        return jnp.where(position < mine, longer, subtotal)

    return lax.fori_loop(0, count - 1, hop, subtotal)


def bucket_of(relative):
    distance = jnp.abs(relative)
    beyond = jnp.full(relative.shape, EXACT, jnp.int32)
    for level_step in range(1, BUCKETS // 2 - EXACT):
        boundary = math.isqrt(EXACT * EXACT * (1 << level_step) - 1) + 1
        beyond = beyond + (distance >= boundary).astype(jnp.int32)
    nearby = jnp.where(distance < EXACT, distance, beyond)
    return nearby + jnp.where(relative > 0, BUCKETS // 2, 0).astype(jnp.int32)


def normalize(values, gain):
    inverse = lax.rsqrt(jnp.mean(values * values, axis=-1, keepdims=True) + 1e-06)
    return (values * inverse * gain, inverse)


def norm_back(values, inverse, gain, upstream):
    scaled_up = upstream * gain
    d_gain = jnp.sum(upstream * values * inverse, axis=0)
    cubed = inverse * inverse * inverse
    d_values = inverse * scaled_up - values * cubed * jnp.mean(
        values * scaled_up, axis=-1, keepdims=True
    )
    return (d_values, d_gain)


def precise(left_side, right_side):
    return jnp.dot(left_side, right_side, precision=lax.Precision.HIGHEST)


def low_dot(left_side, right_side):
    return jnp.dot(left_side, right_side, preferred_element_type=jnp.float32)


def back_dot(left_side, weight):
    return lax.dot_general(
        left_side, weight, (((1,), (1,)), ((), ())), preferred_element_type=jnp.float32
    )


def over_rows(left_side, right_side):
    return lax.dot_general(
        left_side, right_side, (((0,), (0,)), ((), ())), preferred_element_type=jnp.float32
    )


def pair_columns(matrix, pair_index, head_width):
    piece = lax.dynamic_slice_in_dim(matrix, pair_index * 2 * head_width, 2 * head_width, 1)
    return piece.reshape(matrix.shape[0], 2, head_width)


def put_columns(total, piece, pair_index):
    flat_piece = piece.reshape(piece.shape[0], -1)
    return lax.dynamic_update_slice_in_dim(total, flat_piece, pair_index * flat_piece.shape[1], 1)


def put_heads(total, piece, pair_index):
    return lax.dynamic_update_slice_in_dim(total, piece, pair_index * 2, 0)


def unshear(grid_values, row_total, col_total):
    lead_dim = grid_values.shape[0]
    padded = jnp.concatenate(
        [grid_values, jnp.zeros((lead_dim, row_total, row_total - 1), grid_values.dtype)], axis=2
    )
    flat_values = padded.reshape(lead_dim, -1)
    flat_values = jnp.concatenate(
        [
            jnp.zeros((lead_dim, row_total - 1), grid_values.dtype),
            flat_values,
            jnp.zeros((lead_dim, 1), grid_values.dtype),
        ],
        axis=1,
    )
    return jnp.sum(flat_values.reshape(lead_dim, row_total, row_total + col_total), axis=1)[
        :, : row_total + col_total - 1
    ]


def bias_window(table_f, codes):
    one_hot = (
        bucket_of(codes)[:, None] == jnp.arange(table_f.shape[0], dtype=jnp.int32)[None, :]
    ).astype(jnp.float32)
    return (precise(one_hot, table_f).T, one_hot)


def add_counts(earlier, later):
    return earlier + later


def to_experts(received, local_count):
    sources = received.shape[0] // local_count
    shaped = received.reshape(sources, local_count, received.shape[1], received.shape[2])
    return jnp.transpose(shaped, (1, 0, 2, 3)).reshape(
        local_count, sources * received.shape[1], received.shape[2]
    )


def to_sources(by_expert, sources):
    local_count, total_rows, model_width = by_expert.shape
    slot_count = total_rows // sources
    shaped = by_expert.reshape(local_count, sources, slot_count, model_width)
    return jnp.transpose(shaped, (1, 0, 2, 3)).reshape(
        sources * local_count, slot_count, model_width
    )


def attend(query_pair, key_pair, value_pair, bias_pair, key_valid):
    scores = jnp.einsum(
        "qhd,khd->hqk", query_pair, key_pair, preferred_element_type=jnp.float32
    ) + bias_pair.astype(jnp.float32)
    scores = jnp.where(key_valid[None, None, :], scores, -1000000000.0)
    top_score = jnp.max(scores, axis=-1, keepdims=True)
    scaled_exp = jnp.exp(scores - top_score)
    exp_total = jnp.sum(scaled_exp, axis=-1, keepdims=True)
    weights = (scaled_exp / exp_total).astype(jnp.bfloat16)
    attended = jnp.einsum("hqk,khd->qhd", weights, value_pair, preferred_element_type=jnp.float32)
    return (attended, top_score[:, :, 0] + jnp.log(exp_total[:, :, 0]))


def query_side(
    query_pair, key_pair, value_pair, grad_pair, log_norm, bias_pair, key_valid, tok_rows, span_rows
):
    scores = jnp.einsum(
        "qhd,khd->hqk", query_pair, key_pair, preferred_element_type=jnp.float32
    ) + bias_pair.astype(jnp.float32)
    scores = jnp.where(key_valid[None, None, :], scores, -1000000000.0)
    probability = jnp.exp(scores - log_norm[:, :, None])
    d_probs = jnp.einsum("qhd,khd->hqk", grad_pair, value_pair, preferred_element_type=jnp.float32)
    spread = jnp.sum(probability * d_probs, axis=-1)
    d_scores = (probability * (d_probs - spread[:, :, None])).astype(jnp.bfloat16)
    d_query = jnp.einsum("hqk,khd->qhd", d_scores, key_pair, preferred_element_type=jnp.float32)
    d_bias = unshear(d_scores.astype(jnp.float32), tok_rows, span_rows)
    d_key = jnp.einsum("hqk,qhd->khd", d_scores, query_pair, preferred_element_type=jnp.float32)
    d_value = jnp.einsum(
        "hqk,qhd->khd",
        probability.astype(jnp.bfloat16),
        grad_pair,
        preferred_element_type=jnp.float32,
    )
    return (d_query, d_bias, spread, d_key, d_value)


def per_device(
    tokens,
    lengths,
    expert_ids,
    gain_one,
    w_query,
    w_key,
    w_value,
    w_output,
    bias_table,
    gain_two,
    w_router,
    w_in,
    w_out,
    cotangent,
):
    tok_rows, model_width = tokens.shape
    head_count = bias_table.shape[1]
    head_width = model_width // head_count
    pair_count = head_count // 2
    expert_count = w_router.shape[1]
    local_count = w_in.shape[0]
    dp_count = lax.axis_size("dp")
    ex_count = lax.axis_size("expert")
    dp_index = lax.axis_index("dp")
    ex_index = lax.axis_index("expert")
    span_count = dp_count // 2
    block_index = ex_index * dp_count + dp_index
    seq_id = block_index // span_count
    start_row = block_index % span_count * tok_rows
    span_rows = tok_rows * span_count
    bit_count = span_count.bit_length() - 1
    seq_length = jnp.sum(
        jnp.where(jnp.arange(lengths.shape[0], dtype=jnp.int32) == seq_id, lengths, 0)
    )
    valid_mask = start_row + jnp.arange(tok_rows, dtype=jnp.int32) < seq_length
    key_valid = jnp.arange(span_rows, dtype=jnp.int32) < seq_length
    valid_f = valid_mask.astype(jnp.float32)
    table_f = bias_table.astype(jnp.float32)
    window_codes = (
        jnp.arange(span_rows + tok_rows - 1, dtype=jnp.int32) - (tok_rows - 1) - start_row
    )
    window_bias, window_hot = bias_window(table_f, window_codes)
    grid_index = (
        jnp.arange(span_rows, dtype=jnp.int32)[None, :]
        - jnp.arange(tok_rows, dtype=jnp.int32)[:, None]
        + (tok_rows - 1)
    )
    bias_grid = jnp.take(window_bias.astype(jnp.bfloat16), grid_index, axis=1)
    token_f = tokens.astype(jnp.float32)
    gain_a = gain_one.astype(jnp.float32)
    normed_f, inverse_one = normalize(token_f, gain_a)
    normed = normed_f.astype(jnp.bfloat16)
    queries = low_dot(normed, w_query).astype(jnp.bfloat16)
    key_value = jnp.stack([low_dot(normed, w_key), low_dot(normed, w_value)]).astype(jnp.bfloat16)
    held_pair = key_value
    for bit_index in range(bit_count):
        other_pair = partner(held_pair, "dp", bit_index)
        lower_side = dp_index // (1 << bit_index) % 2 == 0
        held_pair = jnp.where(
            lower_side,
            jnp.concatenate([held_pair, other_pair], axis=1),
            jnp.concatenate([other_pair, held_pair], axis=1),
        )
    keys_all = held_pair[0]
    values_all = held_pair[1]

    def forward_pair(pair_index, carry):
        attended_total, log_total = carry
        piece, log_piece = attend(
            pair_columns(queries, pair_index, head_width),
            pair_columns(keys_all, pair_index, head_width),
            pair_columns(values_all, pair_index, head_width),
            lax.dynamic_slice_in_dim(bias_grid, pair_index * 2, 2, 0),
            key_valid,
        )
        return (
            put_columns(attended_total, piece, pair_index),
            put_heads(log_total, log_piece, pair_index),
        )

    attended_f, log_norm = lax.fori_loop(
        0,
        pair_count,
        forward_pair,
        (
            jnp.zeros((tok_rows, model_width), jnp.float32),
            jnp.zeros((head_count, tok_rows), jnp.float32),
        ),
    )
    attended = attended_f.astype(jnp.bfloat16)
    residual = token_f + low_dot(attended, w_output)
    gain_b = gain_two.astype(jnp.float32)
    routed_f, inverse_two = normalize(residual, gain_b)
    routed = routed_f.astype(jnp.bfloat16)
    router = jax.nn.softmax(low_dot(routed, w_router), axis=-1)
    chosen = expert_ids[:, 0]
    chosen_hot = chosen[:, None] == jnp.arange(expert_count, dtype=jnp.int32)[None, :]
    valid_hits = (chosen_hot & valid_mask[:, None]).astype(jnp.int32)
    offsets = carried_in(
        jnp.sum(valid_hits, axis=0), "expert", add_counts, jnp.zeros((expert_count,), jnp.int32)
    )
    local_rank = jnp.sum((jnp.cumsum(valid_hits, axis=0) - valid_hits) * valid_hits, axis=1)
    group_rank = local_rank + jnp.sum(valid_hits * offsets[None, :], axis=1)
    capacity = 5 * tok_rows // (4 * local_count)
    slot_count = 3 * tok_rows // (2 * expert_count)
    kept_mask = valid_mask & (group_rank < capacity)
    target = jnp.where(kept_mask, chosen * slot_count + local_rank, -1)
    placing = (
        jnp.arange(expert_count * slot_count, dtype=jnp.int32)[:, None] == target[None, :]
    ).astype(jnp.bfloat16)
    sending = (
        low_dot(placing, routed).astype(jnp.bfloat16).reshape(expert_count, slot_count, model_width)
    )
    expert_rows = to_experts(
        lax.all_to_all(sending, "expert", split_axis=0, concat_axis=0, tiled=True), local_count
    )
    inner_act = jnp.einsum("erd,edf->erf", expert_rows, w_in, preferred_element_type=jnp.float32)
    active = jax.nn.gelu(inner_act).astype(jnp.bfloat16)
    expert_out = jnp.einsum(
        "erf,efd->erd", active, w_out, preferred_element_type=jnp.float32
    ).astype(jnp.bfloat16)
    returned = lax.all_to_all(
        to_sources(expert_out, ex_count), "expert", split_axis=0, concat_axis=0, tiled=True
    )
    gathered = over_rows(placing, returned.reshape(expert_count * slot_count, model_width))
    kept_f = kept_mask.astype(jnp.float32)
    chosen_f = chosen_hot.astype(jnp.float32)
    chosen_prob = jnp.sum(router * chosen_f, axis=1)
    gate_value = chosen_prob * kept_f
    output = (valid_f[:, None] * (residual + gate_value[:, None] * gathered)).astype(jnp.bfloat16)
    upstream = cotangent.astype(jnp.float32) * valid_f[:, None]
    d_gate = jnp.sum(upstream * gathered, axis=1) * kept_f
    d_expert_tok = (gate_value[:, None] * upstream).astype(jnp.bfloat16)
    d_sending = (
        low_dot(placing, d_expert_tok)
        .astype(jnp.bfloat16)
        .reshape(expert_count, slot_count, model_width)
    )
    d_expert_out = to_experts(
        lax.all_to_all(d_sending, "expert", split_axis=0, concat_axis=0, tiled=True), local_count
    )
    d_active = jnp.einsum("erd,efd->erf", d_expert_out, w_out, preferred_element_type=jnp.float32)
    gelu_slope = jax.vjp(jax.nn.gelu, inner_act)[1]
    d_inner = gelu_slope(d_active)[0].astype(jnp.bfloat16)
    d_w_out = jnp.einsum("erf,erd->efd", active, d_expert_out, preferred_element_type=jnp.float32)
    d_w_in = jnp.einsum("erd,erf->edf", expert_rows, d_inner, preferred_element_type=jnp.float32)
    d_rows = jnp.einsum("erf,edf->erd", d_inner, w_in, preferred_element_type=jnp.float32).astype(
        jnp.bfloat16
    )
    d_back = lax.all_to_all(
        to_sources(d_rows, ex_count), "expert", split_axis=0, concat_axis=0, tiled=True
    )
    d_routed = over_rows(placing, d_back.reshape(expert_count * slot_count, model_width))
    d_logits = router * (chosen_f - chosen_prob[:, None]) * d_gate[:, None]
    d_router = precise(routed.astype(jnp.float32).T, d_logits)
    d_routed = d_routed + precise(d_logits, w_router.astype(jnp.float32).T)
    d_norm_two, d_gain_two = norm_back(residual, inverse_two, gain_b, d_routed)
    d_residual = upstream + d_norm_two
    d_output = precise(attended.astype(jnp.float32).T, d_residual)
    d_attended = precise(d_residual, w_output.astype(jnp.float32).T).astype(jnp.bfloat16)
    bias_span = span_rows + tok_rows - 1
    zero_rows = jnp.zeros((tok_rows, model_width), jnp.float32)
    zero_heads = jnp.zeros((head_count, tok_rows), jnp.float32)
    zero_bias = jnp.zeros((head_count, bias_span), jnp.float32)
    zero_span = jnp.zeros((span_rows, model_width), jnp.float32)

    def backward_pair(pair_index, carry):
        query_total, bias_total, spread_total, key_total, value_total = carry
        d_query_piece, d_bias_piece, spread_piece, d_key_piece, d_value_piece = query_side(
            pair_columns(queries, pair_index, head_width),
            pair_columns(keys_all, pair_index, head_width),
            pair_columns(values_all, pair_index, head_width),
            pair_columns(d_attended, pair_index, head_width),
            lax.dynamic_slice_in_dim(log_norm, pair_index * 2, 2, 0),
            lax.dynamic_slice_in_dim(bias_grid, pair_index * 2, 2, 0),
            key_valid,
            tok_rows,
            span_rows,
        )
        return (
            put_columns(query_total, d_query_piece, pair_index),
            put_heads(bias_total, d_bias_piece, pair_index),
            put_heads(spread_total, spread_piece, pair_index),
            put_columns(key_total, d_key_piece, pair_index),
            put_columns(value_total, d_value_piece, pair_index),
        )

    d_queries_f, d_bias, spread, d_keys_f, d_values_f = lax.fori_loop(
        0, pair_count, backward_pair, (zero_rows, zero_bias, zero_heads, zero_span, zero_span)
    )
    d_held = jnp.stack([d_keys_f, d_values_f])
    for bit_index in reversed(range(bit_count)):
        half_rows = d_held.shape[1] // 2
        upper_side = dp_index // (1 << bit_index) % 2 == 1
        keep_part = jnp.where(upper_side, d_held[:, half_rows:], d_held[:, :half_rows])
        give_part = jnp.where(upper_side, d_held[:, :half_rows], d_held[:, half_rows:])
        d_held = keep_part + partner(give_part.astype(jnp.bfloat16), "dp", bit_index).astype(
            give_part.dtype
        )
    d_key_value = d_held.astype(jnp.bfloat16)
    d_queries = d_queries_f.astype(jnp.bfloat16)
    d_normed = (
        back_dot(d_queries, w_query)
        + back_dot(d_key_value[0], w_key)
        + back_dot(d_key_value[1], w_value)
    )
    d_query = over_rows(normed, d_queries)
    d_key = over_rows(normed, d_key_value[0])
    d_value = over_rows(normed, d_key_value[1])
    d_norm_one, d_gain_one = norm_back(token_f, inverse_one, gain_a, d_normed)
    d_tokens = d_residual + d_norm_one
    d_table = precise(window_hot.T, d_bias.T)
    summed = lax.psum(
        (d_gain_one, d_query, d_key, d_value, d_output, d_table, d_gain_two, d_router),
        ("dp", "expert"),
    )
    d_in, d_out = (
        lax.psum_scatter(d_w_in.astype(jnp.bfloat16), "dp", scatter_dimension=1, tiled=True).astype(
            jnp.float32
        ),
        lax.psum_scatter(
            d_w_out.astype(jnp.bfloat16), "dp", scatter_dimension=1, tiled=True
        ).astype(jnp.float32),
    )
    return (
        output,
        d_tokens,
        summed[0],
        summed[1],
        summed[2],
        summed[3],
        summed[4],
        summed[5],
        summed[6],
        summed[7],
        d_in,
        d_out,
    )


def solution(mesh):
    return jax.shard_map(
        per_device,
        mesh=mesh,
        in_specs=(
            P(("expert", "dp"), None),
            P(),
            P(("expert", "dp"), None),
            P(),
            P(),
            P(),
            P(),
            P(),
            P(),
            P(),
            P(),
            P("expert", None, None),
            P("expert", None, None),
            P(("expert", "dp"), None),
        ),
        out_specs=(
            P(("expert", "dp"), None),
            P(("expert", "dp"), None),
            P(),
            P(),
            P(),
            P(),
            P(),
            P(),
            P(),
            P(),
            P("expert", "dp", None),
            P("expert", "dp", None),
        ),
        check_vma=False,
    )
```

profile of v0, /device:TPU:0, one launch (start us, length us, event | category | flops | bytes accessed | tf_op | source)
XLA Modules:
  0.0 1794.3 jit_solution(2662234196988898298)
XLA Ops:
  20.7 913.3 %gather_fusion = bf16[262144,12]{1,0:T(8,128)(2,1)} fusion(bf16[12,1279]{0,1:T(8,128)(2,1)S(1)} %copy.37, s32[262144]{0:T(1024)S(1)} %broadcast_clamp_fusion), kind=kCustom, calls=%fused_computation | custom fusion | bytes 13631488 | tf_op jit(solution)/shard_map/jit(_take)/gather | solution.py:218
  934.0 54.1 %copy.38 = bf16[256,1024,12]{1,0,2:T(8,128)(2,1)} copy(bf16[256,1024,12]{2,1,0:T(8,128)(2,1)} %bitcast.5) | data formatting | bytes 12582912 | tf_op jit(solution)/shard_map/jit(_take)/gather | solution.py:218
  1009.3 22.1 %collective-permute-done.1 = bf16[2,512,768]{2,1,0:T(8,128)(2,1)} collective-permute-done((bf16[2,512,768]{2,1,0:T(8,128)(2,1)S(1)}, bf16[2,512,768]{2,1,0:T(8,128)(2,1)}, u32[]{:S(2)}, u32[]{:S(2)}) %collective-permute-start.1) | collective-permute-done | bytes 1572896 | tf_op jit(solution)/shard_map/ppermute | solution.py:13
  1041.5 44.4 %while.54 = (s32[]{:T(128)}, bf16[256,768]{0,1:T(8,128)(2,1)}, f32[12,256]{1,0:T(8,128)}, bf16[1024,768]{0,1:T(8,128)(2,1)S(1)}, bf16[256,768]{0,1:T(8,128)(2,1)...) while((s32[]{:T(128)}, bf16[256,768]{0,1:T(8,128)(2,1)}, ...), condition=%wide.region_5.6_spmd.clone, body=%wide.region_2.5_spmd.clone.sunk | while | flops 138936832 | bytes 10373397 | solution.py:251
  1095.8 8.2 all-to-all-done
  1108.5 9.3 all-to-all-done.2
  1119.0 6.9 fusion.91
  1125.8 8.2 fusion.14
  1142.4 7.4 convolution_convert_fusion.5
  1154.2 7.8 convolution_convert_fusion.3
  1190.1 326.0 %while.55 = (s32[]{:T(128)}, bf16[256,768]{0,1:T(8,128)(2,1)}, f32[12,1279]{1,0:T(8,128)}, f32[1024,768]{0,1:T(8,128)}, f32[1024,768]{0,1:T(8,128)}, /*index=5*/...) while((s32[]{:T(128)}, bf16[256,768]{0,1:T(8,128)(2,1)}, ...), condition=%wide.region_22.23_spmd.clone, body=%wide.region_19.22_spmd.clone.sunk | while | flops 342095360 | bytes 59873816 | solution.py:358
  1210.9 25.9 %dynamic-update-slice.8 = f32[2,327680]{1,0:T(2,128)} dynamic-update-slice(f32[2,327680]{1,0:T(2,128)} %dynamic-update-slice.7, f32[2,327424]{1,0:T(2,128)} %reshape.434, s32[]{} %constant.490..sunk, s32[]{} %constant.491..sunk) | dynamic-update-slice | bytes 5238788 | tf_op jit(solution)/shard_map/while
  1265.3 25.9 %dynamic-update-slice.8 = f32[2,327680]{1,0:T(2,128)} dynamic-update-slice(f32[2,327680]{1,0:T(2,128)} %dynamic-update-slice.7, f32[2,327424]{1,0:T(2,128)} %reshape.434, s32[]{} %constant.490..sunk, s32[]{} %constant.491..sunk) | dynamic-update-slice | bytes 5238788 | tf_op jit(solution)/shard_map/while
  1319.5 25.9 %dynamic-update-slice.8 = f32[2,327680]{1,0:T(2,128)} dynamic-update-slice(f32[2,327680]{1,0:T(2,128)} %dynamic-update-slice.7, f32[2,327424]{1,0:T(2,128)} %reshape.434, s32[]{} %constant.490..sunk, s32[]{} %constant.491..sunk) | dynamic-update-slice | bytes 5238788 | tf_op jit(solution)/shard_map/while
  1365.6 6.9 reshape.434
  1373.7 25.9 %dynamic-update-slice.8 = f32[2,327680]{1,0:T(2,128)} dynamic-update-slice(f32[2,327680]{1,0:T(2,128)} %dynamic-update-slice.7, f32[2,327424]{1,0:T(2,128)} %reshape.434, s32[]{} %constant.490..sunk, s32[]{} %constant.491..sunk) | dynamic-update-slice | bytes 5238788 | tf_op jit(solution)/shard_map/while
  1419.8 7.0 reshape.434
  1428.1 25.9 %dynamic-update-slice.8 = f32[2,327680]{1,0:T(2,128)} dynamic-update-slice(f32[2,327680]{1,0:T(2,128)} %dynamic-update-slice.7, f32[2,327424]{1,0:T(2,128)} %reshape.434, s32[]{} %constant.490..sunk, s32[]{} %constant.491..sunk) | dynamic-update-slice | bytes 5238788 | tf_op jit(solution)/shard_map/while
  1474.3 6.9 reshape.434
  1482.5 25.8 %dynamic-update-slice.8 = f32[2,327680]{1,0:T(2,128)} dynamic-update-slice(f32[2,327680]{1,0:T(2,128)} %dynamic-update-slice.7, f32[2,327424]{1,0:T(2,128)} %reshape.434, s32[]{} %constant.490..sunk, s32[]{} %constant.491..sunk) | dynamic-update-slice | bytes 5238788 | tf_op jit(solution)/shard_map/while
  1522.7 34.4 %collective-permute-done.2 = bf16[2,512,768]{1,2,0:T(8,128)(2,1)S(1)} collective-permute-done((bf16[2,512,768]{1,2,0:T(8,128)(2,1)}, bf16[2,512,768]{1,2,0:T(8,128)(2,1)S(1)}, u32[]{:S(2)}, u32[]{:S(2)}) %collective-permute-start.2) | collective-permute-done | bytes 1572896 | tf_op jit(solution)/shard_map/ppermute | solution.py:13
  1568.1 11.6 collective-permute-done.3
  1591.8 42.6 %all-reduce.2 = (f32[768]{0:T(1024)}, f32[32,12]{0,1:T(8,128)}, f32[768]{0:T(1024)}, f32[768,8]{0,1:T(8,128)}) all-reduce(f32[768]{0:T(1024)S(1)} %get-tuple-element.689, f32[32,12]{0,1:T(8,128)S(1)} %copy-done.42, f32[768]{0:T(1024)S(1)} %copy-done.38, f32[768,8]{0,1:T(8,128)S(1)} %copy-done.30), channel_id=1, replica_groups=mesh['dp'=8,'expert'=4] {'dp','expert'}, use_global_device_ids=true, to_apply=%region_25.26 | all-reduce | flops 8064 | bytes 64512 | tf_op jit(solution)/shard_map/psum | solution.py:383
  1642.4 134.2 %all-reduce.6.cloned.1.call-done = (f32[768,768]{1,0:T(8,128)}, f32[768,768]{1,0:T(8,128)}, f32[768,768]{1,0:T(8,128)}, f32[768,768]{1,0:T(8,128)}) async-done(((f32[768,768]{1,0:T(8,128)}, f32[768,768]{1,0:T(8,128)}, f32[768,768]{1,0:T(8,128)}, f32[768,768]{1,0:T(8,128)}), (f32[768,768]{1,0:T(8,128)}, f32[768,768]{1,0:T(8,128)}, f32[768,768]{1,0:T(8,128)}, ...) | async-done | bytes 9437200 | tf_op jit(solution)/shard_map/psum | solution.py:383
  (480 shorter events, 340.1 us)
Async XLA Ops:
  15.2 977.9 %collective-permute-start = (bf16[2,256,768]{2,1,0:T(8,128)(2,1)}, bf16[2,256,768]{2,1,0:T(8,128)(2,1)}, u32[]{:S(2)}, u32[]{:S(2)}) collective-permute-start(bf16[2,256,768]{2,1,0:T(8,128)(2,1)} %pad_maximum_fusion.1), channel_id=1, source_target_pairs={{0,4},{4,0},{8,12},{12,8},{16,20},{20,16},{24,28},{28,24},{1,5},{5... | collective-permute-start | bytes 2359304 | tf_op jit(solution)/shard_map/ppermute | solution.py:13
  934.0 55.0 %copy-start.45 = (bf16[768]{0:T(1024)(128)(2,1)S(1)}, bf16[768]{0:T(1024)(128)(2,1)}, u32[]{:S(2)}) copy-start(bf16[768]{0:T(1024)(128)(2,1)} %param.29) | copy-start | bytes 4612
  934.0 55.0 %copy-start.47 = (s32[8]{0:T(128)S(1)}, s32[8]{0:T(128)}, u32[]{:S(2)}) copy-start(s32[8]{0:T(128)} %param.21) | copy-start | bytes 100
  934.0 56.3 %copy-start.31 = (s32[256,1]{0,1:T(1,128)S(1)}, s32[256,1]{0,1:T(1,128)}, u32[]{:S(2)}) copy-start(s32[256,1]{0,1:T(1,128)} %param.22) | copy-start | bytes 3076
  934.0 57.2 %copy-start.48 = (u32[32]{0:T(128)S(1)}, u32[32]{0:T(128)}, u32[]{:S(2)}) copy-start(u32[32]{0:T(128)} %constant.378) | copy-start | bytes 388
  995.3 36.0 %collective-permute-start.1 = (bf16[2,512,768]{2,1,0:T(8,128)(2,1)S(1)}, bf16[2,512,768]{2,1,0:T(8,128)(2,1)}, u32[]{:S(2)}, u32[]{:S(2)}) collective-permute-start(bf16[2,512,768]{2,1,0:T(8,128)(2,1)S(1)} %maximum_select_fusion.1), channel_id=1, source_target_pairs={{0,8},{4,12},{8,0},{12,4},{16,24},{20,28},{24,16},{28,20},{1,9},{5... | collective-permute-start | bytes 4718600 | tf_op jit(solution)/shard_map/ppermute | solution.py:13
  1089.5 84.6 %copy-start.37 = (f32[256]{0:T(256)}, f32[256]{0:T(256)S(1)}, u32[]{:S(2)}) copy-start(f32[256]{0:T(256)S(1)} %get-tuple-element.771) | copy-start | bytes 3076
  1089.5 84.6 %copy-start.39 = (f32[256]{0:T(256)}, f32[256]{0:T(256)S(1)}, u32[]{:S(2)}) copy-start(f32[256]{0:T(256)S(1)} %fusion.67) | copy-start | bytes 3076
  1089.6 84.6 %copy-start.40 = (f32[256]{0:T(256)}, f32[256]{0:T(256)S(1)}, u32[]{:S(2)}) copy-start(f32[256]{0:T(256)S(1)} %select_reduce_fusion) | copy-start | bytes 3076
  1091.1 13.0 all-to-all-start
  1104.1 13.8 all-to-all-start.2
  1108.2 528.4 %reduce-scatter.5.cloned.1.call-start = ((), (), s32[]{:S(2)}) async-start(), calls=%async_computation.7 | async-start | bytes 10616832 | tf_op jit(solution)/shard_map/reduce_scatter | solution.py:391
  1150.6 17.4 all-to-all-start.1
  1154.1 485.4 %reduce-scatter.3.cloned.1.call-start = ((), (), s32[]{:S(2)}) async-start(), calls=%async_computation.6 | async-start | bytes 10616832 | tf_op jit(solution)/shard_map/reduce_scatter | solution.py:388
  1168.0 13.0 all-to-all-start.3
  1171.5 605.1 %all-reduce.6.cloned.1.call-start = ((), (), s32[]{:S(2)}) async-start(), calls=%async_computation.8 | async-start | bytes 18874368 | tf_op jit(solution)/shard_map/psum | solution.py:383
  1174.1 9.3 copy-start.41
  1520.7 36.5 %collective-permute-start.2 = (bf16[2,512,768]{1,2,0:T(8,128)(2,1)}, bf16[2,512,768]{1,2,0:T(8,128)(2,1)S(1)}, u32[]{:S(2)}, u32[]{:S(2)}) collective-permute-start(bf16[2,512,768]{1,2,0:T(8,128)(2,1)} %select_convert_fusion), channel_id=1, source_target_pairs={{0,8},{4,12},{8,0},{12,4},{16,24},{20,28},{24,16},{28,20},{1,9},{5... | collective-permute-start | bytes 4718600 | tf_op jit(solution)/shard_map/ppermute | solution.py:13
  1522.7 38.8 %copy-start.5 = (bf16[256,768]{1,0:T(8,128)(2,1)S(1)}, bf16[256,768]{1,0:T(8,128)(2,1)}, u32[]{:S(2)}) copy-start(bf16[256,768]{1,0:T(8,128)(2,1)} %param.20) | copy-start | bytes 1179652
  1522.7 38.8 %copy-start.29 = (f32[768]{0:T(1024)S(1)}, f32[768]{0:T(1024)}, u32[]{:S(2)}) copy-start(f32[768]{0:T(1024)} %copy-done.28) | copy-start | bytes 9220
  1522.7 38.8 %copy-start.34 = (f32[256]{0:T(256)S(1)}, f32[256]{0:T(256)}, u32[]{:S(2)}) copy-start(f32[256]{0:T(256)} %copy-done.33) | copy-start | bytes 3076
  1561.0 18.6 %collective-permute-start.3 = (bf16[2,256,768]{1,2,0:T(8,128)(2,1)S(1)}, bf16[2,256,768]{1,2,0:T(8,128)(2,1)S(1)}, u32[]{:S(2)}, u32[]{:S(2)}) collective-permute-start(bf16[2,256,768]{1,2,0:T(8,128)(2,1)S(1)} %select_convert_fusion.1), channel_id=1, source_target_pairs={{0,4},{4,0},{8,12},{12,8},{16,20},{20,16},{24,28},{28,24},{1,5},{5... | collective-permute-start | bytes 2359304 | tf_op jit(solution)/shard_map/ppermute | solution.py:13
  1589.7 44.6 %copy-start.36 = (f32[256]{0:T(256)S(1)}, f32[256]{0:T(256)}, u32[]{:S(2)}) copy-start(f32[256]{0:T(256)} %copy-done.33) | copy-start | bytes 3076
  1589.7 44.6 %copy-start.44 = (f32[256]{0:T(256)S(1)}, f32[256]{0:T(256)}, u32[]{:S(2)}) copy-start(f32[256]{0:T(256)} %get-tuple-element.765) | copy-start | bytes 3076
  (77 other events, 282.7 us)
Sparse Core Ops, SparseCore 0:
  1142.5 162.8 reduce-scatter.4
  1309.4 162.3 reduce-scatter.2
Sparse Core Ops, SparseCore 1:
  1584.2 192.4 all-reduce.5
where the time goes:
time: 1820 us; the launch traced here: 1790 us
  local copies, waits for them, and re-layouts  1280 us (70%)
  waiting for transfers between devices  226 us (12%)
  matrix products  127 us (7%)
  other arithmetic  74.5 us (4%)
  blocking collectives  47.5 us (3%)
  starting transfers between devices  22.2 us (1%)
    gather x2, local copies, waits for them, and re-layouts, per_device(): bias_grid = jnp.take(window_bias.astype(jnp.bfloat16), grid_index, axis=1)  967 us
    while x108, local copies, waits for them, and re-layouts  169 us
    psum x1, waiting for transfers between devices, per_device(): lax.psum((d_gain_one, d_query, d_key, d_value, d_output, d_table, d_gain_...  134 us
    ppermute x4, waiting for transfers between devices, partner(): lax.ppermute(array, axis, [(i, i ^ 1 << apart) for i in range(lax.axis_si...  68.1 us
    psum x1, blocking collectives, per_device(): lax.psum((d_gain_one, d_query, d_key, d_value, d_output, d_table, d_gain_...  42.6 us
    reshape x6, local copies, waits for them, and re-layouts, unshear(): flat_values = padded.reshape(lead_dim, -1)  41.3 us
    dynamic_slice x42, local copies, waits for them, and re-layouts, pair_columns(): lax.dynamic_slice_in_dim(matrix, pair_index * 2 * head_width, 2 * head_wi...  36.6 us
  transfers between devices with their start and end apart: 11, of which 7 were waited for; matrix products, arithmetic and copies ran while one was open for 76% of the time, Pallas kernels for 0%

commit v1 on v0

v1 whole, which is shorter than its diff:
```python
import functools
import math

import jax
import jax.numpy as jnp
from jax import lax
from jax.experimental import pallas as pl
from jax.experimental.pallas import tpu as pltpu
from jax.sharding import PartitionSpec as P

BUCKETS = 32
EXACT = 8
MASKED = -1000000000.0
F32 = jnp.float32
BF16 = jnp.bfloat16
VMEM_BYTES = 56 * 1024 * 1024


def bucket_of(relative):
    distance = jnp.abs(relative)
    beyond = jnp.full(relative.shape, EXACT, jnp.int32)
    for level_step in range(1, BUCKETS // 2 - EXACT):
        boundary = math.isqrt(EXACT * EXACT * (1 << level_step) - 1) + 1
        beyond = beyond + (distance >= boundary).astype(jnp.int32)
    nearby = jnp.where(distance < EXACT, distance, beyond)
    return nearby + jnp.where(relative > 0, BUCKETS // 2, 0).astype(jnp.int32)


def normalize(values, gain):
    inverse = lax.rsqrt(jnp.mean(values * values, axis=-1, keepdims=True) + 1e-06)
    return (values * inverse * gain, inverse)


def norm_back(values, inverse, gain, upstream):
    scaled_up = upstream * gain
    d_gain = jnp.sum(upstream * values * inverse, axis=0)
    cubed = inverse * inverse * inverse
    d_values = inverse * scaled_up - values * cubed * jnp.mean(
        values * scaled_up, axis=-1, keepdims=True
    )
    return (d_values, d_gain)


def dot(left_side, right_side):
    return jnp.dot(left_side, right_side, preferred_element_type=F32)


def dot_t(left_side, right_side):
    return lax.dot_general(
        left_side, right_side, (((1,), (1,)), ((), ())), preferred_element_type=F32
    )


def t_dot(left_side, right_side):
    return lax.dot_general(
        left_side, right_side, (((0,), (0,)), ((), ())), preferred_element_type=F32
    )


def gelu_parts(value):
    scale = math.sqrt(2.0 / math.pi)
    square = value * value
    tanh = jnp.tanh(scale * (value + 0.044715 * value * square))
    half = 0.5 * (1.0 + tanh)
    slope = half + 0.5 * value * (1.0 - tanh * tanh) * scale * (1.0 + 3 * 0.044715 * square)
    return (value * half, slope)


def build_bias(win_ref, bias_ref):
    count, block, _ = bias_ref.shape

    @pl.loop(0, count)
    def _(index):
        row = win_ref[0, pl.ds(index, 1), :]
        wide = jnp.broadcast_to(row, (block, 2 * block))
        bias_ref[index] = pltpu.roll(wide, 0, 1, stride=1, stride_axis=0)[:, :block]


def attend_kernel(length_ref, win_ref, q_ref, k_ref, v_ref, o_ref, lse_ref, bias_ref):
    block = bias_ref.shape[1]
    q_blocks = q_ref.shape[1] // block
    k_blocks = k_ref.shape[1] // block
    build_bias(win_ref, bias_ref)
    length = length_ref[0]

    @pl.loop(0, q_blocks)
    def _(i):
        rows = pl.ds(pl.multiple_of(i * block, block), block)
        query = q_ref[0, rows, :]
        scores = []
        for j in range(k_blocks):
            part = dot_t(k_ref[0, j * block : (j + 1) * block, :], query)
            part = part + bias_ref[j - i + q_blocks - 1]
            position = lax.broadcasted_iota(jnp.int32, (block, 1), 0) + j * block
            scores.append(jnp.where(position < length, part, MASKED))
        top = functools.reduce(jnp.maximum, [jnp.max(s, axis=0, keepdims=True) for s in scores])
        total = jnp.zeros((1, block), F32)
        out = jnp.zeros((v_ref.shape[2], block), F32)
        for j in range(k_blocks):
            scaled = jnp.exp(scores[j] - top)
            total = total + jnp.sum(scaled, axis=0, keepdims=True)
            out = out + t_dot(v_ref[0, j * block : (j + 1) * block, :], scaled.astype(BF16))
        out = out * (1.0 / total)
        o_ref[0, rows, :] = out.T.astype(BF16)
        lse_ref[0, pl.ds(i, 1), :] = top + jnp.log(total)


def attend_back_kernel(
    length_ref, win_ref, q_ref, k_ref, v_ref, g_ref, lse_ref,
    dq_ref, dk_ref, dv_ref, dwin_ref, bias_ref, dbias_ref,
):
    block = bias_ref.shape[1]
    q_blocks = q_ref.shape[1] // block
    k_blocks = k_ref.shape[1] // block
    build_bias(win_ref, bias_ref)
    length = length_ref[0]
    dk_ref[...] = jnp.zeros_like(dk_ref)
    dv_ref[...] = jnp.zeros_like(dv_ref)
    dbias_ref[...] = jnp.zeros_like(dbias_ref)

    @pl.loop(0, q_blocks)
    def _(i):
        rows = pl.ds(pl.multiple_of(i * block, block), block)
        query = q_ref[0, rows, :]
        grad = g_ref[0, rows, :]
        log_norm = lse_ref[0, pl.ds(i, 1), :]
        probs, d_probs = [], []
        spread = jnp.zeros((1, block), F32)
        for j in range(k_blocks):
            keys = slice(j * block, (j + 1) * block)
            part = dot_t(k_ref[0, keys, :], query)
            part = part + bias_ref[j - i + q_blocks - 1]
            position = lax.broadcasted_iota(jnp.int32, (block, 1), 0) + j * block
            part = jnp.where(position < length, part, MASKED)
            prob = jnp.exp(part - log_norm)
            d_prob = dot_t(v_ref[0, keys, :], grad)
            spread = spread + jnp.sum(prob * d_prob, axis=0, keepdims=True)
            dv_ref[0, keys, :] += dot(prob.astype(BF16), grad)
            probs.append(prob)
            d_probs.append(d_prob)
        d_query = jnp.zeros((q_ref.shape[2], block), F32)
        for j in range(k_blocks):
            keys = slice(j * block, (j + 1) * block)
            d_score = probs[j] * (d_probs[j] - spread)
            dbias_ref[j - i + q_blocks - 1] += d_score
            low = d_score.astype(BF16)
            dk_ref[0, keys, :] += dot(low, query)
            d_query = d_query + t_dot(k_ref[0, keys, :], low)
        dq_ref[0, rows, :] = d_query.T.astype(BF16)

    @pl.loop(0, dbias_ref.shape[0])
    def _(index):
        wide = jnp.concatenate([dbias_ref[index], jnp.zeros((block, block), F32)], axis=1)
        half = block // 2
        while half:
            wide = wide[:half] + pltpu.roll(wide[half:], 2 * block - half, 1)
            half //= 2
        dwin_ref[0, pl.ds(index, 1), :] = wide


def head_block(rows, width):
    return pl.BlockSpec((1, rows, width), lambda h: (h, 0, 0))


def attend(length, window, query, key, value):
    heads, q_rows, width = query.shape
    k_rows = key.shape[1]
    count, block = window.shape[1], window.shape[2] // 2
    return pl.pallas_call(
        attend_kernel,
        grid=(heads,),
        in_specs=[
            pl.BlockSpec(memory_space=pltpu.SMEM),
            head_block(count, 2 * block),
            head_block(q_rows, width),
            head_block(k_rows, width),
            head_block(k_rows, width),
        ],
        out_specs=[head_block(q_rows, width), head_block(q_rows // block, block)],
        out_shape=[
            jax.ShapeDtypeStruct((heads, q_rows, width), BF16),
            jax.ShapeDtypeStruct((heads, q_rows // block, block), F32),
        ],
        scratch_shapes=[pltpu.VMEM((count, block, block), F32)],
        compiler_params=pltpu.CompilerParams(vmem_limit_bytes=VMEM_BYTES),
        name="attend",
    )(length, window, query, key, value)


def attend_back(length, window, query, key, value, grad, log_norm):
    heads, q_rows, width = query.shape
    k_rows = key.shape[1]
    count, block = window.shape[1], window.shape[2] // 2
    return pl.pallas_call(
        attend_back_kernel,
        grid=(heads,),
        in_specs=[
            pl.BlockSpec(memory_space=pltpu.SMEM),
            head_block(count, 2 * block),
            head_block(q_rows, width),
            head_block(k_rows, width),
            head_block(k_rows, width),
            head_block(q_rows, width),
            head_block(q_rows // block, block),
        ],
        out_specs=[
            head_block(q_rows, width),
            head_block(k_rows, width),
            head_block(k_rows, width),
            head_block(count, 2 * block),
        ],
        out_shape=[
            jax.ShapeDtypeStruct((heads, q_rows, width), BF16),
            jax.ShapeDtypeStruct((heads, k_rows, width), F32),
            jax.ShapeDtypeStruct((heads, k_rows, width), F32),
            jax.ShapeDtypeStruct((heads, count, 2 * block), F32),
        ],
        scratch_shapes=[pltpu.VMEM((count, block, block), F32) for _ in range(2)],
        compiler_params=pltpu.CompilerParams(vmem_limit_bytes=VMEM_BYTES),
        name="attend_back",
    )(length, window, query, key, value, grad, log_norm)


def experts_kernel(rows_ref, w_in_ref, w_out_ref, out_ref, acc_ref, back_ref):
    width = w_in_ref.shape[1]
    step = pl.program_id(1)

    @pl.when(step == 0)
    def _():
        acc_ref[...] = jnp.zeros_like(acc_ref)
        back_ref[...] = jnp.zeros_like(back_ref)

    inner = dot(rows_ref[0, :, :width], w_in_ref[0])
    active, slope = gelu_parts(inner)
    acc_ref[...] += dot(active.astype(BF16), w_out_ref[0])
    d_active = dot_t(rows_ref[0, :, width:], w_out_ref[0])
    d_inner = (d_active * slope).astype(BF16)
    back_ref[...] += dot_t(d_inner, w_in_ref[0])

    @pl.when(step == pl.num_programs(1) - 1)
    def _():
        out_ref[0, :, :width] = acc_ref[...].astype(BF16)
        out_ref[0, :, width:] = back_ref[...].astype(BF16)


def experts(rows, w_in, w_out):
    local, count, double = rows.shape
    width, hidden = w_in.shape[1:]
    piece = 512
    return pl.pallas_call(
        experts_kernel,
        grid=(local, hidden // piece),
        in_specs=[
            pl.BlockSpec((1, count, double), lambda e, f: (e, 0, 0)),
            pl.BlockSpec((1, width, piece), lambda e, f: (e, 0, f)),
            pl.BlockSpec((1, piece, width), lambda e, f: (e, f, 0)),
        ],
        out_specs=pl.BlockSpec((1, count, double), lambda e, f: (e, 0, 0)),
        out_shape=jax.ShapeDtypeStruct((local, count, double), BF16),
        scratch_shapes=[pltpu.VMEM((count, width), F32) for _ in range(2)],
        compiler_params=pltpu.CompilerParams(vmem_limit_bytes=VMEM_BYTES),
        name="experts",
    )(rows, w_in, w_out)


def weight_grads_kernel(rows_ref, w_in_ref, w_out_ref, d_in_ref, d_out_ref, acc_ref):
    width = w_in_ref.shape[1]
    step = pl.program_id(1)
    rows = rows_ref[...].reshape(rows_ref.shape[0] * rows_ref.shape[2], 2 * width)

    @pl.when(step == 0)
    def _():
        acc_ref[...] = jnp.zeros_like(acc_ref)
        d_out_ref[...] = jnp.zeros_like(d_out_ref)

    inner = dot(rows[:, :width], w_in_ref[0])
    active, slope = gelu_parts(inner)
    d_active = dot_t(rows[:, width:], w_out_ref[0])
    d_inner = (d_active * slope).astype(BF16)
    d_out_ref[0] += t_dot(active.astype(BF16), rows[:, width:])
    acc_ref[...] += t_dot(rows[:, :width], d_inner)

    @pl.when(step == pl.num_programs(1) - 1)
    def _():
        d_in_ref[0] = acc_ref[...].astype(BF16)


def weight_grads(rows, w_in, w_out):
    groups, local, count, double = rows.shape
    width, piece = w_in.shape[1:]
    together = 4
    return pl.pallas_call(
        weight_grads_kernel,
        grid=(local, groups // together),
        in_specs=[
            pl.BlockSpec((together, 1, count, double), lambda e, g: (g, e, 0, 0)),
            pl.BlockSpec((1, width, piece), lambda e, g: (e, 0, 0)),
            pl.BlockSpec((1, piece, width), lambda e, g: (e, 0, 0)),
        ],
        out_specs=[
            pl.BlockSpec((1, width, piece), lambda e, g: (e, 0, 0)),
            pl.BlockSpec((1, piece, width), lambda e, g: (e, 0, 0)),
        ],
        out_shape=[
            jax.ShapeDtypeStruct((local, width, piece), BF16),
            jax.ShapeDtypeStruct((local, piece, width), F32),
        ],
        scratch_shapes=[pltpu.VMEM((width, piece), F32)],
        compiler_params=pltpu.CompilerParams(vmem_limit_bytes=VMEM_BYTES),
        name="weight_grads",
    )(rows, w_in, w_out)


def all_to_all(array, axis, groups=None):
    return lax.all_to_all(
        array, axis, split_axis=0, concat_axis=0, tiled=True, axis_index_groups=groups
    )


def to_experts(received, local):
    total, slots, width = received.shape
    shaped = received.reshape(total // local, local, slots, width)
    return jnp.swapaxes(shaped, 0, 1).reshape(local, total // local * slots, width)


def to_sources(by_expert, sources):
    local, total, width = by_expert.shape
    shaped = by_expert.reshape(local, sources, total // sources, width)
    return jnp.swapaxes(shaped, 0, 1).reshape(sources * local, total // sources, width)


def per_device(
    tokens, lengths, expert_ids, gain_one, w_query, w_key, w_value, w_output,
    bias_table, gain_two, w_router, w_in, w_out, cotangent,
):
    tok_rows, width = tokens.shape
    head_count = bias_table.shape[1]
    head_width = width // head_count
    expert_count = w_router.shape[1]
    local = w_in.shape[0]
    hidden = w_in.shape[2]
    dp_count, ex_count = lax.axis_size("dp"), lax.axis_size("expert")
    dp_index, ex_index = lax.axis_index("dp"), lax.axis_index("expert")
    span = dp_count // 2
    quad = math.gcd(span, head_count)
    heads = head_count // quad
    part = heads * head_width
    q_rows = quad * tok_rows
    q_parts = span // quad
    place = dp_index % span
    mine, q_part = place % quad, place // quad
    quads = [[i * quad + j for j in range(quad)] for i in range(dp_count // quad)]
    spans = [[i * span + j for j in range(span)] for i in range(dp_count // span)]
    seq_id = ex_index * (dp_count // span) + dp_index // span
    start_row = place * tok_rows

    length = jnp.sum(jnp.where(jnp.arange(lengths.shape[0], dtype=jnp.int32) == seq_id, lengths, 0))
    valid_mask = start_row + jnp.arange(tok_rows, dtype=jnp.int32) < length
    valid_f = valid_mask.astype(F32)
    length_arg = length.reshape(1)

    if q_parts == 1:
        tokens_all = all_to_all(
            jnp.broadcast_to(tokens[None], (quad, tok_rows, width)), "dp", quads
        ).reshape(q_rows, width)
        tokens_q = tokens_all
    else:
        tokens_all = lax.all_gather(tokens, "dp", axis_index_groups=spans, tiled=True)
        tokens_q = lax.dynamic_slice_in_dim(tokens_all, q_part * q_rows, q_rows, 0)
    gain_a = gain_one.astype(F32)
    normed_all = normalize(tokens_all.astype(F32), gain_a)[0].astype(BF16)
    normed_q = normalize(tokens_q.astype(F32), gain_a)[0].astype(BF16)

    table = lax.dynamic_slice_in_dim(bias_table.astype(F32), mine * heads, heads, 1)
    counts = span * tok_rows // tok_rows + quad - 1
    offset = jnp.arange(2 * tok_rows, dtype=jnp.int32)
    offset = jnp.where(offset < tok_rows, offset, offset - 2 * tok_rows)
    codes = (
        jnp.arange(counts, dtype=jnp.int32)[:, None] * tok_rows
        - offset[None, :]
        - (q_rows - tok_rows)
        - q_part * q_rows
    )
    window_hot = (
        bucket_of(codes)[:, :, None] == jnp.arange(table.shape[0], dtype=jnp.int32)
    ).astype(BF16)
    window = jnp.einsum("amb,bh->ham", window_hot, table.astype(BF16), preferred_element_type=F32)

    def my_columns(weight):
        return lax.dynamic_slice_in_dim(weight, mine * part, part, 1).reshape(
            width, heads, head_width
        )

    def project(rows, weight):
        return jnp.einsum(
            "sd,dhc->hsc", rows, my_columns(weight), preferred_element_type=F32
        ).astype(BF16)

    query = project(normed_q, w_query)
    key = project(normed_all, w_key)
    value = project(normed_all, w_value)
    attended_heads, log_norm = attend(length_arg, window, query, key, value)
    attended = all_to_all(
        jnp.transpose(
            attended_heads.reshape(heads, quad, tok_rows, head_width), (1, 2, 0, 3)
        ).reshape(quad, tok_rows, part),
        "dp",
        quads,
    )
    attended = jnp.swapaxes(attended, 0, 1).reshape(tok_rows, width)

    token_f = tokens.astype(F32)
    residual = token_f + dot(attended, w_output)
    gain_b = gain_two.astype(F32)
    routed_f, inverse_two = normalize(residual, gain_b)
    routed = routed_f.astype(BF16)
    router = jax.nn.softmax(dot(routed, w_router), axis=-1)

    chosen = expert_ids[:, 0]
    chosen_hot = chosen[:, None] == jnp.arange(expert_count, dtype=jnp.int32)[None, :]
    valid_hits = (chosen_hot & valid_mask[:, None]).astype(jnp.int32)
    per_source = lax.all_gather(jnp.sum(valid_hits, axis=0), "expert")
    earlier = jnp.arange(ex_count, dtype=jnp.int32)[:, None] < ex_index
    offsets = jnp.sum(jnp.where(earlier, per_source, 0), axis=0)
    local_rank = jnp.sum((jnp.cumsum(valid_hits, axis=0) - valid_hits) * valid_hits, axis=1)
    group_rank = local_rank + jnp.sum(valid_hits * offsets[None, :], axis=1)
    capacity = 5 * tok_rows // (4 * local)
    slots = 3 * tok_rows // (2 * expert_count)
    kept_mask = valid_mask & (group_rank < capacity)
    kept_f = kept_mask.astype(F32)
    target = jnp.where(kept_mask, chosen * slots + local_rank, -1)
    placing = (
        jnp.arange(expert_count * slots, dtype=jnp.int32)[:, None] == target[None, :]
    ).astype(BF16)
    chosen_f = chosen_hot.astype(F32)
    chosen_prob = jnp.sum(router * chosen_f, axis=1)
    gate = chosen_prob * kept_f
    upstream = cotangent.astype(F32) * valid_f[:, None]
    d_expert = (gate[:, None] * upstream).astype(BF16)

    sending = dot(placing, jnp.concatenate([routed, d_expert], axis=1)).astype(BF16)
    expert_rows = to_experts(
        all_to_all(sending.reshape(expert_count, slots, 2 * width), "expert"), local
    )
    group_rows = lax.all_gather(expert_rows, "dp")
    results = experts(expert_rows, w_in, w_out)
    returned = all_to_all(to_sources(results, ex_count), "expert")
    gathered = t_dot(placing, returned.reshape(expert_count * slots, 2 * width))
    expert_out, d_routed = gathered[:, :width], gathered[:, width:]

    output = (valid_f[:, None] * (residual + gate[:, None] * expert_out)).astype(BF16)
    d_gate = jnp.sum(upstream * expert_out, axis=1) * kept_f
    d_logits = router * (chosen_f - chosen_prob[:, None]) * d_gate[:, None]
    d_router = t_dot(routed, d_logits.astype(BF16))
    d_routed = d_routed + dot_t(d_logits.astype(BF16), w_router)
    d_norm_two, d_gain_two = norm_back(residual, inverse_two, gain_b, d_routed)
    d_residual = upstream + d_norm_two
    low_residual = d_residual.astype(BF16)
    d_attended = dot_t(low_residual, w_output).astype(BF16)
    d_output = t_dot(attended, low_residual)

    grad = all_to_all(
        jnp.swapaxes(d_attended.reshape(tok_rows, quad, part), 0, 1), "dp", quads
    ).reshape(q_rows, heads, head_width)
    grad = jnp.swapaxes(grad, 0, 1)
    d_query_rows, d_key_rows, d_value_rows, d_window = attend_back(
        length_arg, window, query, key, value, grad, log_norm
    )
    if q_parts > 1:
        strided = [
            [i * span + j + quad * n for n in range(q_parts)]
            for i in range(dp_count // span)
            for j in range(quad)
        ]
        d_key_rows, d_value_rows = [
            lax.psum_scatter(
                rows, "dp", scatter_dimension=1, axis_index_groups=strided, tiled=True
            )
            for rows in (d_key_rows, d_value_rows)
        ]
    d_rows = jnp.stack([d_query_rows, d_key_rows.astype(BF16), d_value_rows.astype(BF16)])
    d_parts = jnp.einsum("sd,khsc->dkhc", normed_q, d_rows, preferred_element_type=F32)
    d_table = jnp.einsum("amb,ham->bh", window_hot.astype(F32), d_window, precision="highest")
    d_mine = all_to_all(
        jnp.transpose(
            d_rows.reshape(3, heads, quad, tok_rows, head_width), (2, 3, 0, 1, 4)
        ).reshape(quad, tok_rows, 3 * part),
        "dp",
        quads,
    ).reshape(quad, tok_rows, 3, part)
    d_mine = jnp.transpose(d_mine, (2, 1, 0, 3)).reshape(3, tok_rows, width)
    d_normed = dot_t(d_mine[0], w_query) + dot_t(d_mine[1], w_key) + dot_t(d_mine[2], w_value)
    inverse_one = normalize(token_f, gain_a)[1]
    d_norm_one, d_gain_one = norm_back(token_f, inverse_one, gain_a, d_normed)
    d_tokens = d_residual + d_norm_one

    piece = hidden // dp_count
    my_in = lax.dynamic_slice_in_dim(w_in, dp_index * piece, piece, 2)
    my_out = lax.dynamic_slice_in_dim(w_out, dp_index * piece, piece, 1)
    d_in_piece, d_out = weight_grads(group_rows, my_in, my_out)
    d_in = all_to_all(
        jnp.swapaxes(d_in_piece.reshape(local, dp_count, width // dp_count, piece), 0, 1), "dp"
    )
    d_in = (
        jnp.transpose(d_in, (1, 2, 0, 3)).reshape(local, width // dp_count, hidden).astype(F32)
    )

    def spread(array, axis):
        wide = jnp.zeros(array.shape[:axis] + (array.shape[axis] * quad,) + array.shape[axis + 1 :], F32)
        return lax.dynamic_update_slice_in_dim(wide, array, mine * array.shape[axis], axis)

    d_parts = d_parts.reshape(width, 3, part)
    big = jnp.stack([spread(d_parts[:, n], 1) for n in range(3)] + [d_output])
    summed = lax.psum(big.astype(BF16), ("dp", "expert")).astype(F32)
    small = lax.psum(
        (d_gain_one, spread(d_table, 1), d_gain_two, d_router), ("dp", "expert")
    )
    return (
        output, d_tokens, small[0], summed[0], summed[1], summed[2], summed[3],
        small[1], small[2], small[3], d_in, d_out,
    )


def solution(mesh):
    rows = P(("expert", "dp"), None)
    owned = P("expert", None, None)
    return jax.shard_map(
        per_device,
        mesh=mesh,
        in_specs=(
            rows, P(), rows, P(), P(), P(), P(), P(), P(), P(), P(), owned, owned, rows,
        ),
        out_specs=(
            rows, rows, P(), P(), P(), P(), P(), P(), P(), P(),
            P("expert", "dp", None), P("expert", "dp", None),
        ),
        check_vma=False,
    )
```

time: 1820 us -> 415 us (0.23); the launches traced: 1790 us -> 413 us
  local copies, waits for them, and re-layouts: 1280 us -> 66.6 us
  waiting for transfers between devices: 226 us -> 94.2 us
  matrix products: 127 us -> 14.4 us
  Pallas kernels: 0 us -> 83.8 us
  other arithmetic: 74.5 us -> 25.8 us
  blocking collectives: 47.5 us -> 90.4 us
    gather x2 -> x0, local copies, waits for them, and re-layouts: 967 us -> none  [per_device(): bias_grid = jnp.take(window_bias.astype(jnp.bfloat16), grid_index, axis=1)]
    while x108 -> x0, local copies, waits for them, and re-layouts: 169 us -> none
    dot_general x69 -> x17, matrix products: 127 us -> 14.4 us  [the longest x5 3.3 us: dot_t(): lax.dot_general(left_side, right_side, (((1,), (1,)), ((), ())), preferre...]
    pallas_call x0 -> x4, Pallas kernels: none -> 83.8 us  [the longest x1 33.7 us: attend_back(): pl.pallas_call(attend_back_kernel, grid=(heads,), in_specs=[pl.BlockSpec(...]
    ppermute x4 -> x0, waiting for transfers between devices: 68.1 us -> none  [partner(): lax.ppermute(array, axis, [(i, i ^ 1 << apart) for i in range(lax.axis_si...]
    psum x1, waiting for transfers between devices: 134 us -> 69.5 us  [per_device(): summed = lax.psum(big.astype(BF16), ('dp', 'expert')).astype(F32)]
    reshape x10 -> x5, local copies, waits for them, and re-layouts: 44.1 us -> 7.44 us  [the longest x1 2.48 us: per_device(): d_in_piece.reshape(local, dp_count, width // dp_count, piece)]
    all_to_all x0 -> x2, blocking collectives: none -> 36.6 us  [all_to_all(): lax.all_to_all(array, axis, split_axis=0, concat_axis=0, tiled=True, axis...]
  transfers between devices with their start and end apart: 11 -> 7, of which waited for: 7 -> 4; matrix products, arithmetic and copies ran while one was open for 76% -> 19% of each run, Pallas kernels for 0% -> 16%
where the time goes in v1:
time: 415 us; the launch traced here: 413 us
  waiting for transfers between devices  94.2 us (23%)
  blocking collectives  90.4 us (22%)
  Pallas kernels  83.8 us (20%)
  local copies, waits for them, and re-layouts  66.6 us (16%)
  other arithmetic  25.8 us (6%)
  starting transfers between devices  20.9 us (5%)
  between operations  17 us (4%)
  matrix products  14.4 us (3%)
    psum x1, waiting for transfers between devices, per_device(): summed = lax.psum(big.astype(BF16), ('dp', 'expert')).astype(F32)  69.5 us
    psum x1, blocking collectives, per_device(): lax.psum((d_gain_one, spread(d_table, 1), d_gain_two, d_router), ('dp', '...  48.9 us
    all_to_all x2, blocking collectives, all_to_all(): lax.all_to_all(array, axis, split_axis=0, concat_axis=0, tiled=True, axis...  36.6 us
    pallas_call x1, Pallas kernels, attend_back(): pl.pallas_call(attend_back_kernel, grid=(heads,), in_specs=[pl.BlockSpec(...  33.7 us
    all_to_all x5, starting transfers between devices, all_to_all(): lax.all_to_all(array, axis, split_axis=0, concat_axis=0, tiled=True, axis...  20.8 us
    pallas_call x1, Pallas kernels, experts(): pl.pallas_call(experts_kernel, grid=(local, hidden // piece), in_specs=[p...  18.5 us
    pallas_call x1, Pallas kernels, attend(): pl.pallas_call(attend_kernel, grid=(heads,), in_specs=[pl.BlockSpec(memor...  15.8 us
    pallas_call x1, Pallas kernels, weight_grads(): pl.pallas_call(weight_grads_kernel, grid=(local, groups // together), in_...  15.8 us
  transfers between devices with their start and end apart: 7, of which 4 were waited for; matrix products, arithmetic and copies ran while one was open for 19% of the time, Pallas kernels for 16%

profile of v1, /device:TPU:0, one launch (start us, length us, event | category | flops | bytes accessed | tf_op | source)
XLA Modules:
  0.0 413.0 jit_solution(15725701611738440696)
XLA Ops:
  10.4 5.4 %all-to-all-start = ((bf16[4,256,768]{2,1,0:T(8,128)(2,1)}), bf16[4,256,768]{2,1,0:T(8,128)(2,1)S(1)}, u32[]{:S(2)}, u32[]{:S(2)}) async-start(bf16[4,256,768]{2,1,0:T(8,128)(2,1)} %broadcast_in_dim.24), calls=%async_computation | async-start | bytes 3145728 | tf_op jit(solution)/shard_map/all_to_all | solution.py:315
  26.5 8.5 %all-to-all-done = bf16[4,256,768]{2,1,0:T(8,128)(2,1)S(1)} async-done(((bf16[4,256,768]{2,1,0:T(8,128)(2,1)}), bf16[4,256,768]{2,1,0:T(8,128)(2,1)S(1)}, u32[]{:S(2)}, u32[]{:S(2)}) %all-to-all-start) | async-done | bytes 1572896 | tf_op jit(solution)/shard_map/all_to_all | solution.py:315
  45.6 15.8 %attend.1 = (bf16[3,1024,64]{2,1,0:T(8,128)(2,1)}, f32[3,4,256]{2,1,0:T(4,128)}) custom-call(s32[1]{0:T(128)} %bitcast.length_ref, f32[3,7,512]{2,1,0:T(8,128)} %copy.117.win_ref, bf16[3,1024,64]{2,1,0:T(8,128)(2,1)} %bitcast.119, bf16[3,1024,64]{2,1,0:T(8,128)(2,1)} %bitcast.121, bf16[3,1024,64]{2,1,0:T(8,128)(2,1)} %bitcast.123), custom_call_target="tpu_custom_call" | custom-call | tf_op jit(solution)/shard_map/attend/pallas_call | solution.py:169
  63.7 3.5 all-to-all-start.1
  68.8 4.9 %all-reduce = s32[32]{0:T(128)S(1)} all-reduce(s32[32]{0:T(128)S(1)} %dynamic-update-slice), channel_id=2, replica_groups=mesh['dp'=8,'expert'=4] {'expert'}, use_global_device_ids=true, to_apply=%add | all-reduce | flops 32 | bytes 256
  79.9 18.3 %all_to_all.35 = bf16[8,48,1536]{2,1,0:T(8,128)(2,1)S(1)} all-to-all(bf16[8,48,1536]{2,1,0:T(8,128)(2,1)S(1)} %bitcast.146), channel_id=1, replica_groups=mesh['dp'=8,'expert'=4] {'expert'}, dimensions={0} | all-to-all | bytes 2359296 | tf_op jit(solution)/shard_map/all_to_all | solution.py:315
  99.3 18.5 %experts.1 = bf16[2,192,1536]{2,1,0:T(8,128)(2,1)} custom-call(bf16[2,192,1536]{2,1,0:T(8,128)(2,1)} %bitcast.118, bf16[2,768,3072]{2,1,0:T(8,128)(2,1)} %w_in_ref.1, bf16[2,3072,768]{2,1,0:T(8,128)(2,1)} %w_out_ref.1), custom_call_target="tpu_custom_call" | custom-call | tf_op jit(solution)/shard_map/experts/pallas_call | solution.py:250
  119.2 18.3 %all_to_all.36 = bf16[8,48,1536]{2,1,0:T(8,128)(2,1)S(1)} all-to-all(bf16[8,48,1536]{2,1,0:T(8,128)(2,1)S(1)} %bitcast.128), channel_id=1, replica_groups=mesh['dp'=8,'expert'=4] {'expert'}, dimensions={0} | all-to-all | bytes 2359296 | tf_op jit(solution)/shard_map/all_to_all | solution.py:315
  143.4 4.2 %all-to-all-start.4 = ((bf16[4,256,192]{1,2,0:T(8,128)(2,1)}), bf16[4,256,192]{1,2,0:T(8,128)(2,1)S(1)}, u32[]{:S(2)}, u32[]{:S(2)}) async-start(bf16[4,256,192]{1,2,0:T(8,128)(2,1)} %bitcast.30), calls=%async_computation.4 | async-start | bytes 786432 | tf_op jit(solution)/shard_map/all_to_all | solution.py:315
  150.0 2.5 constant_dynamic-slice_fusion.w_out_ref
  156.4 33.7 %attend_back.1 = (bf16[3,1024,64]{2,1,0:T(8,128)(2,1)}, f32[3,1024,64]{2,1,0:T(8,128)}, f32[3,1024,64]{2,1,0:T(8,128)}, f32[3,7,512]{2,1,0:T(8,128)}) custom-call(s32[1]{0:T(128)} %bitcast.length_ref, f32[3,7,512]{2,1,0:T(8,128)} %copy.117.win_ref, bf16[3,1024,64]{2,1,0:T(8,128)(2,1)} %bitcast.120, bf16[3,1024,64]{2,1,0:T(8,128)(2,1)} %bitcast.122, ...), custom_call_target="tpu_custom_call" | custom-call | tf_op jit(solution)/shard_map/attend_back/pallas_call | solution.py:194
  198.8 4.3 %all-to-all-start.5 = ((bf16[4,256,576]{1,2,0:T(8,128)(2,1)}), bf16[4,256,576]{1,2,0:T(8,128)(2,1)}, u32[]{:S(2)}, u32[]{:S(2)}) async-start(bf16[4,256,576]{1,2,0:T(8,128)(2,1)} %bitcast.126), calls=%async_computation.5 | async-start | bytes 2359296 | tf_op jit(solution)/shard_map/all_to_all | solution.py:315
  208.1 3.8 copy.128
  215.0 3.9 dynamic_update_slice.15
  221.0 4.6 %dynamic_update_slice.17 = bf16[1,768,768]{2,1,0:T(8,128)(2,1)} dynamic-update-slice(bf16[1,768,768]{2,1,0:T(8,128)(2,1)} %stack.43.clone, bf16[1,768,192]{2,1,0:T(8,128)(2,1)S(1)} %copy.131, s32[]{:T(128)} %constant.94.clone.1, s32[]{:T(128)} %constant.94.clone.1, s32[]{:T(128)S(6)} %select_n.83) | dynamic-update-slice | bytes 589828 | tf_op jit(solution)/shard_map/dynamic_update_slice | solution.py:510
  225.6 3.9 dynamic_update_slice.16
  229.6 3.6 pad_maximum_fusion
  235.0 15.5 %all-gather.3.cloned.1.call-done.rows_ref = bf16[8,2,192,1536]{3,2,1,0:T(8,128)(2,1)} async-done(((bf16[1,2,192,1536]{3,2,1,0:T(8,128)(2,1)}), bf16[8,2,192,1536]{3,2,1,0:T(8,128)(2,1)}) %all-gather.3.cloned.1.call-update) | async-done | bytes 9437200 | tf_op jit(solution)/shard_map/all_gather | solution.py:445
  250.5 15.8 %weight_grads.1 = (bf16[2,768,384]{2,1,0:T(8,128)(2,1)}, f32[2,384,768]{2,1,0:T(8,128)}) custom-call(bf16[8,2,192,1536]{3,2,1,0:T(8,128)(2,1)} %all-gather.3.cloned.1.call-done.rows_ref, bf16[2,768,384]{2,1,0:T(8,128)(2,1)} %constant_dynamic-slice_fusion.1.w_in_ref, bf16[2,384,768]{2,1,0:T(8,128)(2,1)} %constant_dynamic-slice_fusion.w_out_ref), custom_call_target="tpu_custom_call" | custom-call | tf_op jit(solution)/shard_map/weight_grads/pallas_call | solution.py:292
  268.8 3.6 all-to-all-start.6
  277.1 48.9 %all-reduce.1 = (f32[768]{0:T(1024)}, f32[32,12]{0,1:T(8,128)}, f32[768]{0:T(1024)}, f32[768,8]{0,1:T(8,128)}) all-reduce(f32[768]{0:T(1024)S(1)} %get-tuple-element.30, f32[32,12]{0,1:T(8,128)S(1)} %dynamic_update_slice.18, f32[768]{0:T(1024)S(1)} %copy-done.42, ...), channel_id=1, replica_groups=mesh['dp'=8,'expert'=4] {'dp','expert'}, use_global_device_ids=true, to_apply=%region_17.18 | all-reduce | flops 8064 | bytes 64512 | tf_op jit(solution)/shard_map/psum | solution.py:515
  327.1 69.5 %all-reduce.4.cloned.1.call-done = bf16[4,768,768]{2,1,0:T(8,128)(2,1)} async-done(((bf16[4,768,768]{2,1,0:T(8,128)(2,1)}), bf16[4,768,768]{2,1,0:T(8,128)(2,1)}) %all-reduce.4.cloned.1.call-update) | async-done | bytes 4718608 | tf_op jit(solution)/shard_map/psum | solution.py:514
  396.6 3.2 convert_element_type.198
  399.8 3.8 slice_bitcast_fusion
  (226 shorter events, 78.2 us)
Async XLA Ops:
  8.0 67.4 %copy-start = (bf16[768,768]{1,0:T(8,128)(2,1)S(1)}, bf16[768,768]{1,0:T(8,128)(2,1)}, u32[]{:S(2)}) copy-start(bf16[768,768]{1,0:T(8,128)(2,1)} %param.21) | copy-start | bytes 3538948
  10.4 5.4 %copy-start.56 = (bf16[768]{0:T(1024)(128)(2,1)S(1)}, bf16[768]{0:T(1024)(128)(2,1)}, u32[]{:S(2)}) copy-start(bf16[768]{0:T(1024)(128)(2,1)} %param.17) | copy-start | bytes 4612
  10.4 5.4 %copy-start.59 = (s32[8]{0:T(128)S(1)}, s32[8]{0:T(128)}, u32[]{:S(2)}) copy-start(s32[8]{0:T(128)} %param.15) | copy-start | bytes 100
  10.4 6.6 %copy-start.22 = (s32[256,1]{0,1:T(1,128)S(1)}, s32[256,1]{0,1:T(1,128)}, u32[]{:S(2)}) copy-start(s32[256,1]{0,1:T(1,128)} %param.16) | copy-start | bytes 3076
  10.4 24.6 %all-to-all-start = ((bf16[4,256,768]{2,1,0:T(8,128)(2,1)}), bf16[4,256,768]{2,1,0:T(8,128)(2,1)S(1)}, u32[]{:S(2)}, u32[]{:S(2)}) async-start(bf16[4,256,768]{2,1,0:T(8,128)(2,1)} %broadcast_in_dim.24), calls=%async_computation | async-start | bytes 3145728 | tf_op jit(solution)/shard_map/all_to_all | solution.py:315
  61.4 5.7 %copy-start.49 = (pred[256]{0:T(512)(128)(4,1)S(1)}, pred[256]{0:T(512)(128)(4,1)}, u32[]{:S(2)}) copy-start(pred[256]{0:T(512)(128)(4,1)} %get-tuple-element.41) | copy-start | bytes 772
  61.4 5.9 %copy-start.60 = (u32[32]{0:T(128)S(1)}, u32[32]{0:T(128)}, u32[]{:S(2)}) copy-start(u32[32]{0:T(128)} %constant.128) | copy-start | bytes 388
  61.4 12.4 %copy-start.57 = (bf16[768]{0:T(1024)(128)(2,1)S(1)}, bf16[768]{0:T(1024)(128)(2,1)}, u32[]{:S(2)}) copy-start(bf16[768]{0:T(1024)(128)(2,1)} %param.23) | copy-start | bytes 4612
  61.5 12.4 %copy-start.55 = (s32[8,2]{0,1:T(2,128)S(1)}, s32[8,2]{0,1:T(2,128)}, u32[]{:S(2)}) copy-start(s32[8,2]{0,1:T(2,128)} %slice_reduce_fusion) | copy-start | bytes 196
  61.5 12.5 %copy-start.23 = (s32[256,1]{0,1:T(1,128)S(1)}, s32[256,1]{0,1:T(1,128)}, u32[]{:S(2)}) copy-start(s32[256,1]{0,1:T(1,128)} %param.16) | copy-start | bytes 3076
  63.7 11.0 %all-to-all-start.1 = ((bf16[4,256,192]{1,2,0:T(8,128)(2,1)}), bf16[4,256,192]{1,2,0:T(8,128)(2,1)S(1)}, u32[]{:S(2)}, u32[]{:S(2)}) async-start(bf16[4,256,192]{1,2,0:T(8,128)(2,1)} %bitcast.13), calls=%async_computation.1 | async-start | bytes 786432 | tf_op jit(solution)/shard_map/all_to_all | solution.py:315
  67.1 183.4 %all-gather.3.cloned.1.call-start = ((), (), s32[]{:S(2)}) async-start(), calls=%async_computation.8 | async-start | bytes 10616832 | tf_op jit(solution)/shard_map/all_gather | solution.py:445
  75.4 3.1 copy-start.27
  75.4 3.4 copy-start.24
  75.4 3.4 copy-start.50
  75.4 3.5 copy-start.13
  75.4 3.5 copy-start.32
  119.2 18.3 %copy-start.53 = (s32[256]{0:T(256)S(1)}, s32[256]{0:T(256)}, u32[]{:S(2)}) copy-start(s32[256]{0:T(256)} %get-tuple-element.38) | copy-start | bytes 3076
  143.4 11.2 %all-to-all-start.4 = ((bf16[4,256,192]{1,2,0:T(8,128)(2,1)}), bf16[4,256,192]{1,2,0:T(8,128)(2,1)S(1)}, u32[]{:S(2)}, u32[]{:S(2)}) async-start(bf16[4,256,192]{1,2,0:T(8,128)(2,1)} %bitcast.30), calls=%async_computation.4 | async-start | bytes 786432 | tf_op jit(solution)/shard_map/all_to_all | solution.py:315
  150.0 2.5 copy-start.10
  198.8 70.0 %all-to-all-start.5 = ((bf16[4,256,576]{1,2,0:T(8,128)(2,1)}), bf16[4,256,576]{1,2,0:T(8,128)(2,1)}, u32[]{:S(2)}, u32[]{:S(2)}) async-start(bf16[4,256,576]{1,2,0:T(8,128)(2,1)} %bitcast.126), calls=%async_computation.5 | async-start | bytes 2359296 | tf_op jit(solution)/shard_map/all_to_all | solution.py:315
  203.1 193.5 %all-reduce.4.cloned.1.call-start = ((), (), s32[]{:S(2)}) async-start(), calls=%async_computation.7 | async-start | bytes 9437184 | tf_op jit(solution)/shard_map/psum | solution.py:514
  221.0 8.6 %copy-start.7 = (bf16[1,768,768]{2,1,0:T(8,128)(2,1)S(1)}, bf16[1,768,768]{2,1,0:T(8,128)(2,1)}, u32[]{:S(2)}) copy-start(bf16[1,768,768]{2,1,0:T(8,128)(2,1)} %fusion.3) | copy-start | bytes 3538948
  268.8 134.8 %all-to-all-start.6 = ((bf16[8,2,96,384]{3,2,1,0:T(8,128)(2,1)}), bf16[8,2,96,384]{3,2,1,0:T(8,128)(2,1)S(1)}, u32[]{:S(2)}, u32[]{:S(2)}) async-start(bf16[8,2,96,384]{3,2,1,0:T(8,128)(2,1)} %bitcast.112), calls=%async_computation.6 | async-start | bytes 2359296 | tf_op jit(solution)/shard_map/all_to_all | solution.py:315
  (44 other events, 52.1 us)
Sparse Core Ops, SparseCore 0:
  99.4 151.0 all-gather.2
Sparse Core Ops, SparseCore 1:
  233.4 163.1 all-reduce.3

commit v2 on v1

--- a/solution.py
+++ b/solution.py
@@ -311,6 +311,423 @@
     )(rows, w_in, w_out)
 
 
+class Place:
+    def __init__(self):
+        dp, ex = lax.axis_index("dp"), lax.axis_index("expert")
+        self.y = lax.rem(dp, 2)
+        self.z_lo = lax.rem(lax.div(dp, 2), 2)
+        self.z_hi = lax.div(dp, 4)
+        self.core = lax.rem(ex, 2)
+        self.x = lax.div(ex, 2)
+
+    def member(self):
+        return self.z_lo * 2 + self.y
+
+    def flip(self, **bits):
+        c = {n: getattr(self, n) for n in ("y", "z_lo", "z_hi", "core", "x")}
+        for name in bits:
+            c[name] = 1 - c[name]
+        return (c["z_hi"] * 4 + c["z_lo"] * 2 + c["y"], c["x"] * 2 + c["core"])
+
+    def relation(self, r):
+        bits = {}
+        if r % 2:
+            bits["y"] = 1
+        if r // 2:
+            bits["z_lo"] = 1
+        y = 1 - self.y if r % 2 else self.y
+        z_lo = 1 - self.z_lo if r // 2 else self.z_lo
+        return self.flip(**bits), z_lo * 2 + y
+
+
+def send(src, dst, send_sem, recv_sem, device):
+    copy = pltpu.make_async_remote_copy(
+        src_ref=src, dst_ref=dst, send_sem=send_sem, recv_sem=recv_sem,
+        device_id=device, device_id_type=pl.DeviceIdType.MESH,
+    )
+    copy.start()
+    return copy
+
+
+def greet(devices):
+    barrier = pltpu.get_barrier_semaphore()
+    for device in devices:
+        pl.semaphore_signal(barrier, inc=1, device_id=device, device_id_type=pl.DeviceIdType.MESH)
+    pl.semaphore_wait(barrier, len(devices))
+
+
+def attend_quad_kernel(length_ref, win_ref, qkv_ref, o_ref, lse_ref, bias_ref):
+    heads = win_ref.shape[0]
+    block = bias_ref.shape[1]
+    part = qkv_ref.shape[1] // 3
+    width = part // heads
+    blocks = qkv_ref.shape[0] // block
+    length = length_ref[0]
+    for h in range(heads):
+        fill_bias(win_ref, h, bias_ref)
+        cols = slice(h * width, (h + 1) * width)
+        key = qkv_ref[:, part + h * width : part + (h + 1) * width]
+        value = qkv_ref[:, 2 * part + h * width : 2 * part + (h + 1) * width]
+
+        @pl.loop(0, blocks)
+        def _(i):
+            rows = pl.ds(pl.multiple_of(i * block, block), block)
+            query = qkv_ref[rows, cols]
+            scores = []
+            for j in range(blocks):
+                piece = dot_t(key[j * block : (j + 1) * block], query)
+                piece = piece + bias_ref[j - i + blocks - 1]
+                position = lax.broadcasted_iota(jnp.int32, (block, 1), 0) + j * block
+                scores.append(jnp.where(position < length, piece, MASKED))
+            top = functools.reduce(
+                jnp.maximum, [jnp.max(s, axis=0, keepdims=True) for s in scores]
+            )
+            total = jnp.zeros((1, block), F32)
+            out = jnp.zeros((width, block), F32)
+            for j in range(blocks):
+                scaled = jnp.exp(scores[j] - top)
+                total = total + jnp.sum(scaled, axis=0, keepdims=True)
+                out = out + t_dot(value[j * block : (j + 1) * block], scaled.astype(BF16))
+            out = out * (1.0 / total)
+            o_ref[rows, cols] = out.T.astype(BF16)
+            lse_ref[h, pl.ds(i, 1), :] = top + jnp.log(total)
+
+
+def fill_bias(win_ref, h, bias_ref):
+    count, block, _ = bias_ref.shape
+
+    @pl.loop(0, count)
+    def _(index):
+        wide = jnp.broadcast_to(win_ref[h, pl.ds(index, 1), :], (block, 2 * block))
+        bias_ref[index] = pltpu.roll(wide, 0, 1, stride=1, stride_axis=0)[:, :block]
+
+
+def attend_quad(length, window, qkv):
+    heads, count, double = window.shape
+    block = double // 2
+    rows, triple = qkv.shape
+    return pl.pallas_call(
+        attend_quad_kernel,
+        in_specs=[pl.BlockSpec(memory_space=pltpu.SMEM)] + [pl.BlockSpec(memory_space=pltpu.VMEM)] * 2,
+        out_specs=[pl.BlockSpec(memory_space=pltpu.VMEM)] * 2,
+        out_shape=[
+            jax.ShapeDtypeStruct((rows, triple // 3), BF16),
+            jax.ShapeDtypeStruct((heads, rows // block, block), F32),
+        ],
+        scratch_shapes=[pltpu.VMEM((count, block, block), F32)],
+        compiler_params=pltpu.CompilerParams(vmem_limit_bytes=VMEM_BYTES),
+        name="attend_quad",
+    )(length, window, qkv)
+
+
+def back_kernel(
+    length_ref, win_ref, hot_ref, qkv_ref, lse_ref, attended_ref, normed_ref, token_ref,
+    gain_ref, residual_ref, w_output_ref, w_quad_ref, small_ref,
+    d_tokens_ref, d_weights_ref, total_ref,
+    grad_ref, grad_send, low_ref, bias_ref, dbias_ref, dkey_ref, dvalue_ref, dqkv_ref,
+    dmine_ref, load_ref, first_ref, second_ref, third_ref, sum_one_ref, sum_two_ref, all_ref,
+    small_send, small_recv,
+    grad_sems, low_sems, mine_sems, first_sems, second_sems, third_sems, ring_sems, core_sems,
+    small_sems,
+):
+    place = Place()
+    mine = place.member()
+    heads = win_ref.shape[0]
+    block = bias_ref.shape[1]
+    part = qkv_ref.shape[1] // 3
+    width = part // heads
+    blocks = qkv_ref.shape[0] // block
+    quad = blocks
+    full = normed_ref.shape[1]
+    length = length_ref[0]
+
+    def my_rows(index):
+        return pl.ds(pl.multiple_of(index * block, block), block)
+
+    others = [place.relation(r) for r in (1, 2, 3)]
+    greet(
+        [device for device, _ in others]
+        + [place.flip(core=1), place.flip(x=1), place.flip(z_hi=1)]
+    )
+
+    low = residual_ref[...].astype(BF16)
+    low_ref[my_rows(mine), :] = low
+    d_attended = dot_t(low, w_output_ref[...]).astype(BF16)
+    for m in range(quad):
+        grad_send[m] = d_attended[:, m * part : (m + 1) * part]
+    copies = []
+    for n, (device, member) in enumerate(others):
+        copies.append(
+            send(grad_send.at[member], grad_ref.at[my_rows(mine)], grad_sems.at[0, n], grad_sems.at[1, n], device)
+        )
+    low_copies = []
+    for n, (device, member) in enumerate(others):
+        low_copies.append(
+            send(low_ref.at[my_rows(mine)], low_ref.at[my_rows(mine)], low_sems.at[0, n], low_sems.at[1, n], device)
+        )
+    grad_ref[my_rows(mine), :] = grad_send[mine]
+    fill_bias(win_ref, 0, bias_ref)
+    for copy in copies:
+        copy.wait()
+
+    for h in range(heads):
+        if h:
+            fill_bias(win_ref, h, bias_ref)
+        cols = slice(h * width, (h + 1) * width)
+        key = qkv_ref[:, part + h * width : part + (h + 1) * width]
+        value = qkv_ref[:, 2 * part + h * width : 2 * part + (h + 1) * width]
+        dkey_ref[...] = jnp.zeros_like(dkey_ref)
+        dvalue_ref[...] = jnp.zeros_like(dvalue_ref)
+        dbias_ref[...] = jnp.zeros_like(dbias_ref)
+
+        @pl.loop(0, blocks)
+        def _(i):
+            rows = my_rows(i)
+            query = qkv_ref[rows, cols]
+            grad = grad_ref[rows, cols]
+            log_norm = lse_ref[h, pl.ds(i, 1), :]
+            probs, d_probs = [], []
+            spread = jnp.zeros((1, block), F32)
+            for j in range(blocks):
+                keys = slice(j * block, (j + 1) * block)
+                piece = dot_t(key[keys], query)
+                piece = piece + bias_ref[j - i + blocks - 1]
+                position = lax.broadcasted_iota(jnp.int32, (block, 1), 0) + j * block
+                piece = jnp.where(position < length, piece, MASKED)
+                prob = jnp.exp(piece - log_norm)
+                d_prob = dot_t(value[keys], grad)
+                spread = spread + jnp.sum(prob * d_prob, axis=0, keepdims=True)
+                dvalue_ref[keys, :] += dot(prob.astype(BF16), grad)
+                probs.append(prob)
+                d_probs.append(d_prob)
+            d_query = jnp.zeros((width, block), F32)
+            for j in range(blocks):
+                keys = slice(j * block, (j + 1) * block)
+                d_score = probs[j] * (d_probs[j] - spread)
+                dbias_ref[j - i + blocks - 1] += d_score
+                low_score = d_score.astype(BF16)
+                dkey_ref[keys, :] += dot(low_score, query)
+                d_query = d_query + t_dot(key[keys], low_score)
+            dqkv_ref[rows, cols] = d_query.T.astype(BF16)
+
+        dqkv_ref[:, part + h * width : part + (h + 1) * width] = dkey_ref[...].astype(BF16)
+        dqkv_ref[:, 2 * part + h * width : 2 * part + (h + 1) * width] = dvalue_ref[...].astype(BF16)
+        table_row = jnp.zeros((1, hot_ref.shape[2]), F32)
+        for a in range(dbias_ref.shape[0]):
+            wide = jnp.concatenate([dbias_ref[a], jnp.zeros((block, block), F32)], axis=1)
+            half = block // 2
+            while half:
+                wide = wide[:half] + pltpu.roll(wide[half:], 2 * block - half, 1)
+                half //= 2
+            table_row = table_row + jnp.dot(
+                wide, hot_ref[a], precision=lax.Precision.HIGHEST, preferred_element_type=F32
+            )
+        if h == 0:
+            small_send[0] = small_ref[...]
+        for m in range(quad):
+            row = 12 + m * heads + h
+            small_send[0, row : row + 1, : hot_ref.shape[2]] = jnp.where(mine == m, table_row, 0.0)
+
+    mine_copies = []
+    for n, (device, member) in enumerate(others):
+        mine_copies.append(
+            send(dqkv_ref.at[my_rows(member)], dmine_ref.at[mine], mine_sems.at[0, n], mine_sems.at[1, n], device)
+        )
+    dmine_ref[mine] = dqkv_ref[my_rows(mine), :]
+
+    d_parts = t_dot(normed_ref[...], dqkv_ref[...])
+    d_gain = lax.dot_general(
+        jnp.ones((8, 3 * part), F32), d_parts * w_quad_ref[mine].astype(F32), (((1,), (1,)), ((), ())),
+        precision=lax.Precision.HIGHEST, preferred_element_type=F32,
+    )
+    load_ref[:, : 3 * part] = d_parts.astype(BF16)
+    gain = gain_ref[...]
+    small_send[0, 0:1, :] = d_gain[0:1] / gain
+    for copy in low_copies:
+        copy.wait()
+    d_output = t_dot(attended_ref[...], low_ref[...]).astype(BF16)
+    for m in range(quad):
+        load_ref[m * part : (m + 1) * part, 3 * part :] = d_output[:, m * part : (m + 1) * part]
+
+    core, x = place.core, place.x
+    quarter = load_ref.shape[0] // 4
+
+    def chunk(c, b):
+        return pl.ds(pl.multiple_of((c * 2 + b) * quarter, quarter), quarter)
+
+    core_device, x_device, z_device = (
+        place.flip(core=1), place.flip(x=1), place.flip(z_hi=1),
+    )
+    one = [
+        send(load_ref.at[chunk(1 - core, 1 - x)], first_ref.at[0], first_sems.at[0, 0], first_sems.at[1, 0], core_device),
+        send(load_ref.at[chunk(1 - core, x)], first_ref.at[1], first_sems.at[0, 1], first_sems.at[1, 1], core_device),
+    ]
+    small_devices = [core_device, x_device, z_device, others[0][0], others[1][0]]
+    small_copies = []
+
+    def small_start(n):
+        small_copies.append(
+            send(small_send.at[n], small_recv.at[n], small_sems.at[0, n], small_sems.at[1, n], small_devices[n])
+        )
+
+    def small_end(n):
+        small_copies[n].wait()
+        total = small_send[n] + small_recv[n]
+        if n + 1 < len(small_devices):
+            small_send[n + 1] = total
+        else:
+            total_ref[...] = total
+
+    small_start(0)
+
+    for copy in mine_copies:
+        copy.wait()
+    d_normed = dot_t(dmine_ref[0], w_quad_ref[0])
+    for m in range(1, quad):
+        d_normed = d_normed + dot_t(dmine_ref[m], w_quad_ref[m])
+
+    one[0].wait()
+    sum_one_ref[...] = (load_ref[chunk(core, 1 - x), :].astype(F32) + first_ref[0].astype(F32)).astype(BF16)
+    two = send(sum_one_ref, second_ref, second_sems.at[0], second_sems.at[1], x_device)
+    small_end(0)
+    small_start(1)
+    token = token_ref[...].astype(F32)
+    inverse = lax.rsqrt(jnp.mean(token * token, axis=-1, keepdims=True) + 1e-06)
+    scaled = d_normed * gain
+    cubed = inverse * inverse * inverse
+    d_tokens_ref[...] = residual_ref[...] + inverse * scaled - token * cubed * jnp.mean(
+        token * scaled, axis=-1, keepdims=True
+    )
+    one[1].wait()
+    two.wait()
+    sum_two_ref[...] = (
+        load_ref[chunk(core, x), :].astype(F32) + first_ref[1].astype(F32) + second_ref[...].astype(F32)
+    ).astype(BF16)
+    three = send(sum_two_ref, third_ref, third_sems.at[0], third_sems.at[1], z_device)
+    small_end(1)
+    small_start(2)
+    three.wait()
+    all_ref[mine, chunk(core, x), :] = (sum_two_ref[...].astype(F32) + third_ref[...].astype(F32)).astype(BF16)
+
+    thirds = 3
+    third = quarter // thirds
+    steps = {"x": x_device, "y": others[0][0], "z": others[1][0]}
+
+    def spot(axes, t):
+        y = 1 - place.y if "y" in axes else place.y
+        z_lo = 1 - place.z_lo if "z" in axes else place.z_lo
+        xx = 1 - x if "x" in axes else x
+        row = pl.multiple_of((core * 2 + xx) * quarter + t * third, third)
+        return all_ref.at[z_lo * 2 + y, pl.ds(row, third)]
+
+    orders = ("xyz", "yzx", "zxy")
+    passed = []
+
+    def to_core(axes, t, n):
+        where = spot(axes, t)
+        passed.append(send(where, where, core_sems.at[0, t, n], core_sems.at[1, t, n], core_device))
+
+    rings = {}
+
+    def forward(axes, t, axis, n):
+        where = spot(axes, t)
+        rings[t, n] = send(where, where, ring_sems.at[0, t, n], ring_sems.at[1, t, n], steps[axis])
+
+    for t, (a, b, c) in enumerate(orders):
+        forward("", t, a, 0)
+        forward("", t, b, 1)
+        forward("", t, c, 3)
+        to_core("", t, 0)
+    small_end(2)
+    small_start(3)
+    for t, (a, b, c) in enumerate(orders):
+        rings[t, 0].wait_recv()
+        forward(a, t, b, 2)
+        forward(a, t, c, 4)
+        to_core(a, t, 1)
+    small_end(3)
+    small_start(4)
+    for t, (a, b, c) in enumerate(orders):
+        rings[t, 1].wait_recv()
+        forward(b, t, c, 5)
+        to_core(b, t, 2)
+        rings[t, 2].wait_recv()
+        forward(a + b, t, c, 6)
+        to_core(a + b, t, 3)
+    small_end(4)
+    for t, (a, b, c) in enumerate(orders):
+        for n, axes in ((3, c), (4, a + c), (5, b + c), (6, a + b + c)):
+            rings[t, n].wait_recv()
+            to_core(axes, t, n + 1)
+    for t in range(thirds):
+        for n in range(7):
+            rings[t, n].wait_send()
+    for copy in passed:
+        copy.wait()
+
+    @pl.loop(0, full // 64)
+    def _(i):
+        rows = pl.ds(pl.multiple_of(i * 64, 64), 64)
+        for kind in range(3):
+            d_weights_ref[kind, rows, :] = jnp.concatenate(
+                [all_ref[m, rows, kind * part : (kind + 1) * part].astype(F32) for m in range(quad)], axis=1
+            )
+
+    for m in range(quad):
+        d_weights_ref[3, m * part : (m + 1) * part, :] = jnp.concatenate(
+            [all_ref[m, n * part : (n + 1) * part, 3 * part :].astype(F32) for n in range(quad)], axis=1
+        )
+
+
+def back(length, window, hot, qkv, log_norm, attended, normed, tokens, gain, residual, w_output, w_quad, small):
+    heads, count, double = window.shape
+    block = double // 2
+    rows, triple = qkv.shape
+    part = triple // 3
+    full = normed.shape[1]
+    width = part // heads
+    quad = rows // block
+    quarter = full // 4
+    vmem = pl.BlockSpec(memory_space=pltpu.VMEM)
+    dma = pltpu.SemaphoreType.DMA
+    return pl.pallas_call(
+        back_kernel,
+        in_specs=[pl.BlockSpec(memory_space=pltpu.SMEM)] + [vmem] * 12,
+        out_specs=[vmem] * 3,
+        out_shape=[
+            jax.ShapeDtypeStruct((block, full), F32),
+            jax.ShapeDtypeStruct((4, full, full), F32),
+            jax.ShapeDtypeStruct(small.shape, F32),
+        ],
+        scratch_shapes=[
+            pltpu.VMEM((rows, part), BF16),
+            pltpu.VMEM((quad, block, part), BF16),
+            pltpu.VMEM((rows, full), BF16),
+            pltpu.VMEM((count, block, block), F32),
+            pltpu.VMEM((count, block, block), F32),
+            pltpu.VMEM((rows, width), F32),
+            pltpu.VMEM((rows, width), F32),
+            pltpu.VMEM((rows, triple), BF16),
+            pltpu.VMEM((quad, block, triple), BF16),
+            pltpu.VMEM((full, full), BF16),
+            pltpu.VMEM((2, quarter, full), BF16),
+            pltpu.VMEM((quarter, full), BF16),
+            pltpu.VMEM((quarter, full), BF16),
+            pltpu.VMEM((quarter, full), BF16),
+            pltpu.VMEM((quarter, full), BF16),
+            pltpu.VMEM((quad, full, full), BF16),
+            pltpu.VMEM((5,) + small.shape, F32),
+            pltpu.VMEM((5,) + small.shape, F32),
+            dma((2, 3)), dma((2, 3)), dma((2, 3)), dma((2, 2)), dma((2,)), dma((2,)),
+            dma((2, 3, 7)), dma((2, 3, 8)), dma((2, 5)),
+        ],
+        compiler_params=pltpu.CompilerParams(
+            vmem_limit_bytes=VMEM_BYTES, collective_id=0, has_side_effects=True
+        ),
+        name="back",
+    )(length, window, hot, qkv, log_norm, attended, normed, tokens, gain, residual, w_output, w_quad, small)
+
+
 def all_to_all(array, axis, groups=None):
     return lax.all_to_all(
         array, axis, split_axis=0, concat_axis=0, tiled=True, axis_index_groups=groups
@@ -521,11 +938,139 @@
     )
 
 
+def per_device_quad(
+    tokens, lengths, expert_ids, gain_one, w_query, w_key, w_value, w_output,
+    bias_table, gain_two, w_router, w_in, w_out, cotangent,
+):
+    tok_rows, width = tokens.shape
+    head_count = bias_table.shape[1]
+    expert_count = w_router.shape[1]
+    local = w_in.shape[0]
+    hidden = w_in.shape[2]
+    dp_count, ex_count = lax.axis_size("dp"), lax.axis_size("expert")
+    dp_index, ex_index = lax.axis_index("dp"), lax.axis_index("expert")
+    quad = dp_count // 2
+    heads = head_count // quad
+    part = width // quad
+    q_rows = quad * tok_rows
+    mine = dp_index % quad
+    quads = [[i * quad + j for j in range(quad)] for i in range(dp_count // quad)]
+    seq_id = ex_index * 2 + dp_index // quad
+    start_row = mine * tok_rows
+
+    length = jnp.sum(jnp.where(jnp.arange(lengths.shape[0], dtype=jnp.int32) == seq_id, lengths, 0))
+    valid_mask = start_row + jnp.arange(tok_rows, dtype=jnp.int32) < length
+    valid_f = valid_mask.astype(F32)
+    length_arg = length.reshape(1)
+
+    tokens_all = all_to_all(
+        jnp.broadcast_to(tokens[None], (quad, tok_rows, width)), "dp", quads
+    ).reshape(q_rows, width)
+    gain_a = gain_one.astype(F32)
+    normed = normalize(tokens_all.astype(F32), gain_a)[0].astype(BF16)
+
+    table = lax.dynamic_slice_in_dim(bias_table, mine * heads, heads, 1)
+    counts = 2 * quad - 1
+    offset = jnp.arange(2 * tok_rows, dtype=jnp.int32)
+    offset = jnp.where(offset < tok_rows, offset, offset - 2 * tok_rows)
+    codes = (
+        jnp.arange(counts, dtype=jnp.int32)[:, None] * tok_rows
+        - offset[None, :]
+        - (q_rows - tok_rows)
+    )
+    window_hot = (
+        bucket_of(codes)[:, :, None] == jnp.arange(table.shape[0], dtype=jnp.int32)
+    ).astype(F32)
+    window = jnp.einsum(
+        "amb,bh->ham", window_hot.astype(BF16), table, preferred_element_type=F32
+    )
+
+    w_quad = jnp.transpose(
+        jnp.stack([w.reshape(width, quad, part) for w in (w_query, w_key, w_value)], axis=1),
+        (2, 0, 1, 3),
+    ).reshape(quad, width, 3 * part)
+    w_mine = lax.dynamic_index_in_dim(w_quad, mine, 0, keepdims=False)
+    qkv = dot(normed, w_mine).astype(BF16)
+    attended_heads, log_norm = attend_quad(length_arg, window, qkv)
+    attended = all_to_all(attended_heads.reshape(quad, tok_rows, part), "dp", quads)
+    attended = jnp.swapaxes(attended, 0, 1).reshape(tok_rows, width)
+
+    token_f = tokens.astype(F32)
+    residual = token_f + dot(attended, w_output)
+    gain_b = gain_two.astype(F32)
+    routed_f, inverse_two = normalize(residual, gain_b)
+    routed = routed_f.astype(BF16)
+    router = jax.nn.softmax(dot(routed, w_router), axis=-1)
+
+    chosen = expert_ids[:, 0]
+    chosen_hot = chosen[:, None] == jnp.arange(expert_count, dtype=jnp.int32)[None, :]
+    valid_hits = (chosen_hot & valid_mask[:, None]).astype(jnp.int32)
+    per_source = lax.all_gather(jnp.sum(valid_hits, axis=0), "expert")
+    earlier = jnp.arange(ex_count, dtype=jnp.int32)[:, None] < ex_index
+    offsets = jnp.sum(jnp.where(earlier, per_source, 0), axis=0)
+    local_rank = jnp.sum((jnp.cumsum(valid_hits, axis=0) - valid_hits) * valid_hits, axis=1)
+    group_rank = local_rank + jnp.sum(valid_hits * offsets[None, :], axis=1)
+    capacity = 5 * tok_rows // (4 * local)
+    slots = 3 * tok_rows // (2 * expert_count)
+    kept_mask = valid_mask & (group_rank < capacity)
+    kept_f = kept_mask.astype(F32)
+    target = jnp.where(kept_mask, chosen * slots + local_rank, -1)
+    placing = (
+        jnp.arange(expert_count * slots, dtype=jnp.int32)[:, None] == target[None, :]
+    ).astype(BF16)
+    chosen_f = chosen_hot.astype(F32)
+    chosen_prob = jnp.sum(router * chosen_f, axis=1)
+    gate = chosen_prob * kept_f
+    upstream = cotangent.astype(F32) * valid_f[:, None]
+    d_expert = (gate[:, None] * upstream).astype(BF16)
+
+    sending = dot(placing, jnp.concatenate([routed, d_expert], axis=1)).astype(BF16)
+    expert_rows = to_experts(
+        all_to_all(sending.reshape(expert_count, slots, 2 * width), "expert"), local
+    )
+    group_rows = lax.all_gather(expert_rows, "dp")
+    results = experts(expert_rows, w_in, w_out)
+    returned = all_to_all(to_sources(results, ex_count), "expert")
+    gathered = t_dot(placing, returned.reshape(expert_count * slots, 2 * width))
+    expert_out, d_routed = gathered[:, :width], gathered[:, width:]
+
+    output = (valid_f[:, None] * (residual + gate[:, None] * expert_out)).astype(BF16)
+    d_gate = jnp.sum(upstream * expert_out, axis=1) * kept_f
+    d_logits = (router * (chosen_f - chosen_prob[:, None]) * d_gate[:, None]).astype(BF16)
+    d_router = t_dot(d_logits, routed)
+    d_routed = d_routed + dot_t(d_logits, w_router)
+    d_norm_two, d_gain_two = norm_back(residual, inverse_two, gain_b, d_routed)
+    d_residual = upstream + d_norm_two
+    blank = jnp.zeros((1, width), F32)
+    small = jnp.concatenate([blank, d_gain_two[None], d_router] + [blank] * (2 + head_count))
+
+    d_tokens, d_weights, total = back(
+        length_arg, window, window_hot, qkv, log_norm, attended_heads, normed, tokens,
+        gain_a[None], d_residual, w_output, w_quad, small,
+    )
+
+    piece = hidden // dp_count
+    my_in = lax.dynamic_slice_in_dim(w_in, dp_index * piece, piece, 2)
+    my_out = lax.dynamic_slice_in_dim(w_out, dp_index * piece, piece, 1)
+    group_rows, d_tokens = lax.optimization_barrier((group_rows, d_tokens))
+    d_in_piece, d_out = weight_grads(group_rows, my_in, my_out)
+    d_in = all_to_all(
+        jnp.swapaxes(d_in_piece.reshape(local, dp_count, width // dp_count, piece), 0, 1), "dp"
+    )
+    d_in = (
+        jnp.transpose(d_in, (1, 2, 0, 3)).reshape(local, width // dp_count, hidden).astype(F32)
+    )
+    return (
+        output, d_tokens, total[0], d_weights[0], d_weights[1], d_weights[2], d_weights[3],
+        total[12:, : table.shape[0]].T, total[1], total[2 : 2 + expert_count].T, d_in, d_out,
+    )
+
+
 def solution(mesh):
     rows = P(("expert", "dp"), None)
     owned = P("expert", None, None)
     return jax.shard_map(
-        per_device,
+        per_device_quad if dict(mesh.shape) == {"dp": 8, "expert": 4} else per_device,
         mesh=mesh,
         in_specs=(
             rows, P(), rows, P(), P(), P(), P(), P(), P(), P(), P(), owned, owned, rows,

time: 415 us -> 369 us (0.89)
  Pallas kernels: 83.8 us -> 217 us
  waiting for transfers between devices: 94.2 us -> 22.8 us
  blocking collectives: 90.4 us -> 23.2 us
  local copies, waits for them, and re-layouts: 66.6 us -> 48.2 us
  other arithmetic: 25.8 us -> 14.5 us
  matrix products: 14.4 us -> 9.69 us
  starting transfers between devices: 20.9 us -> 16.3 us
    pallas_call x2, Pallas kernels: 49.6 us -> 183 us  [the longest x1 165 us: back(): pl.pallas_call(back_kernel, in_specs=[pl.BlockSpec(memory_space=pltpu.SME...]
    psum x1 -> x0, waiting for transfers between devices: 69.5 us -> none  [per_device(): summed = lax.psum(big.astype(BF16), ('dp', 'expert')).astype(F32)]
    psum x1 -> x0, blocking collectives: 48.9 us -> none  [per_device(): lax.psum((d_gain_one, spread(d_table, 1), d_gain_two, d_router), ('dp', '...]
    all_to_all x2 -> x1, blocking collectives: 36.6 us -> 18.3 us  [all_to_all(): lax.all_to_all(array, axis, split_axis=0, concat_axis=0, tiled=True, axis...]
    all_gather x1, waiting for transfers between devices: 15.5 us -> 0.02 us  [per_device_quad(): group_rows = lax.all_gather(expert_rows, 'dp')]
    all_to_all x5 -> x4, waiting for transfers between devices: 9.14 us -> 22.8 us  [all_to_all(): lax.all_to_all(array, axis, split_axis=0, concat_axis=0, tiled=True, axis...]
    dynamic_update_slice x4 -> x0, local copies, waits for them, and re-layouts: 12.5 us -> none  [spread(): lax.dynamic_update_slice_in_dim(wide, array, mine * array.shape[axis], axis)]
    another operation x6 -> x2, other arithmetic: 8.25 us -> 0.62 us  [the longest x3 3.99 us: per_device(): jnp.stack([d_query_rows, d_key_rows.astype(BF16), d_value_rows.astype(BF1...]
  transfers between devices with their start and end apart: 7 -> 5, of which waited for: 4 -> 2; matrix products, arithmetic and copies ran while one was open for 19% -> 14% of each run, Pallas kernels for 16% -> 50%
where the time goes in v2:
time: 369 us; the launch traced here: 367 us
  Pallas kernels  217 us (59%)
  local copies, waits for them, and re-layouts  48.2 us (13%)
  blocking collectives  23.2 us (6%)
  waiting for transfers between devices  22.8 us (6%)
  starting transfers between devices  16.3 us (4%)
  between operations  15.3 us (4%)
  other arithmetic  14.5 us (4%)
  matrix products  9.69 us (3%)
    pallas_call x1, Pallas kernels, back(): pl.pallas_call(back_kernel, in_specs=[pl.BlockSpec(memory_space=pltpu.SME...  165 us
    all_to_all x4, waiting for transfers between devices, all_to_all(): lax.all_to_all(array, axis, split_axis=0, concat_axis=0, tiled=True, axis...  22.8 us
    pallas_call x1, Pallas kernels, experts(): pl.pallas_call(experts_kernel, grid=(local, hidden // piece), in_specs=[p...  18.5 us
    all_to_all x1, blocking collectives, all_to_all(): lax.all_to_all(array, axis, split_axis=0, concat_axis=0, tiled=True, axis...  18.3 us
    pallas_call x1, Pallas kernels, attend_quad(): pl.pallas_call(attend_quad_kernel, in_specs=[pl.BlockSpec(memory_space=pl...  17.6 us
    all_to_all x4, starting transfers between devices, all_to_all(): lax.all_to_all(array, axis, split_axis=0, concat_axis=0, tiled=True, axis...  16.2 us
    pallas_call x1, Pallas kernels, weight_grads(): pl.pallas_call(weight_grads_kernel, grid=(local, groups // together), in_...  15.7 us
    unnamed x90, local copies, waits for them, and re-layouts  10.7 us
  transfers between devices with their start and end apart: 5, of which 2 were waited for; matrix products, arithmetic and copies ran while one was open for 14% of the time, Pallas kernels for 50%

profile of v2, /device:TPU:0, one launch (start us, length us, event | category | flops | bytes accessed | tf_op | source)
XLA Modules:
  0.0 367.2 jit_solution(7329425063337628890)
XLA Ops:
  7.2 2.2 broadcast_in_dim.32
  9.4 5.4 %all-to-all-start = ((bf16[4,256,768]{2,1,0:T(8,128)(2,1)}), bf16[4,256,768]{2,1,0:T(8,128)(2,1)S(1)}, u32[]{:S(2)}, u32[]{:S(2)}) async-start(bf16[4,256,768]{2,1,0:T(8,128)(2,1)} %broadcast_in_dim.32), calls=%async_computation | async-start | bytes 3145728 | tf_op jit(solution)/shard_map/all_to_all | solution.py:732
  16.4 2.4 copy.63
  18.8 2.4 copy.64
  23.0 2.1 copy.65
  31.2 2.9 all-to-all-done
  35.5 3.7 convolution_convert_fusion.1.qkv_ref
  39.2 17.6 %attend_quad.1 = (bf16[1024,192]{1,0:T(8,128)(2,1)}, f32[3,4,256]{2,1,0:T(4,128)}) custom-call(s32[1]{0:T(128)} %bitcast.length_ref, f32[3,7,512]{2,1,0:T(8,128)} %copy.67.win_ref, bf16[1024,576]{1,0:T(8,128)(2,1)} %convolution_convert_fusion.1.qkv_ref), custom_call_target="tpu_custom_call" | custom-call | tf_op jit(solution)/shard_map/attend_quad/pallas_call | solution.py:409
  56.8 2.0 copy.68
  58.8 3.5 all-to-all-start.1
  64.0 4.9 %all-reduce = s32[32]{0:T(128)S(1)} all-reduce(s32[32]{0:T(128)S(1)} %dynamic-update-slice), channel_id=2, replica_groups=mesh['dp'=8,'expert'=4] {'expert'}, use_global_device_ids=true, to_apply=%add | all-reduce | flops 32 | bytes 256
  74.9 18.3 %all_to_all.25 = bf16[8,48,1536]{2,1,0:T(8,128)(2,1)S(1)} all-to-all(bf16[8,48,1536]{2,1,0:T(8,128)(2,1)S(1)} %bitcast.90), channel_id=1, replica_groups=mesh['dp'=8,'expert'=4] {'expert'}, dimensions={0} | all-to-all | bytes 2359296 | tf_op jit(solution)/shard_map/all_to_all | solution.py:732
  94.4 18.5 %experts.1 = bf16[2,192,1536]{2,1,0:T(8,128)(2,1)} custom-call(bf16[2,192,1536]{2,1,0:T(8,128)(2,1)} %bitcast.77, bf16[2,768,3072]{2,1,0:T(8,128)(2,1)} %w_in_ref.1, bf16[2,3072,768]{2,1,0:T(8,128)(2,1)} %w_out_ref.1), custom_call_target="tpu_custom_call" | custom-call | tf_op jit(solution)/shard_map/experts/pallas_call | solution.py:250
  112.9 2.4 copy.70
  115.3 3.7 %all-to-all-start.3 = ((bf16[8,48,1536]{2,1,0:T(8,128)(2,1)}), bf16[8,48,1536]{2,1,0:T(8,128)(2,1)S(1)}, u32[]{:S(2)}, u32[]{:S(2)}) async-start(bf16[8,48,1536]{2,1,0:T(8,128)(2,1)} %bitcast.82), calls=%async_computation.3 | async-start | bytes 2359296 | tf_op jit(solution)/shard_map/all_to_all | solution.py:732
  119.0 5.9 %copy.73.w_quad_ref = bf16[4,768,576]{2,1,0:T(8,128)(2,1)} copy(bf16[4,768,576]{1,2,0:T(8,128)(2,1)} %bitcast.75) | data formatting | bytes 7077888 | tf_op jit(solution)/shard_map/reshape | solution.py:991
  127.4 2.4 constant_dynamic-slice_fusion.w_out_ref
  129.8 2.4 constant_dynamic-slice_fusion.1.w_in_ref
  140.9 165.5 %back.1 = (f32[256,768]{1,0:T(8,128)}, f32[4,768,768]{2,1,0:T(8,128)}, f32[24,768]{1,0:T(8,128)}) custom-call(s32[1]{0:T(128)} %bitcast.length_ref, f32[3,7,512]{2,1,0:T(8,128)} %copy.67.win_ref, f32[7,512,32]{2,1,0:T(8,128)} %fusion.2.hot_ref, bf16[1024,576]{1,0:T(8,128)(2,1)} %convolution_convert_fusion.1.qkv_ref, f32[3,4,256]{2,1,0:T(4,128)} %get-tuple-element.22.lse_ref, ...), custom_call_target="tpu_custom_call" | custom-call | tf_op jit(solution)/shard_map/back/pallas_call | solution.py:693
  306.4 15.7 %weight_grads.1 = (bf16[2,768,384]{2,1,0:T(8,128)(2,1)}, f32[2,384,768]{2,1,0:T(8,128)}) custom-call(bf16[8,2,192,1536]{3,2,1,0:T(8,128)(2,1)} %all-gather.3.cloned.1.call-done.rows_ref, bf16[2,768,384]{2,1,0:T(8,128)(2,1)} %constant_dynamic-slice_fusion.1.w_in_ref, bf16[2,384,768]{2,1,0:T(8,128)(2,1)} %constant_dynamic-slice_fusion.w_out_ref), custom_call_target="tpu_custom_call" | custom-call | tf_op jit(solution)/shard_map/weight_grads/pallas_call | solution.py:292
  322.1 2.4 copy.81
  324.6 3.7 %all-to-all-start.4 = ((bf16[8,2,96,384]{3,2,1,0:T(8,128)(2,1)}), bf16[8,2,96,384]{3,2,1,0:T(8,128)(2,1)S(1)}, u32[]{:S(2)}, u32[]{:S(2)}) async-start(bf16[8,2,96,384]{3,2,1,0:T(8,128)(2,1)} %bitcast.73), calls=%async_computation.4 | async-start | bytes 2359296 | tf_op jit(solution)/shard_map/all_to_all | solution.py:732
  330.1 7.6 %slice_bitcast_fusion = (f32[768,768]{1,0:T(8,128)}, f32[768,768]{1,0:T(8,128)}, f32[768,768]{1,0:T(8,128)}, f32[768,768]{1,0:T(8,128)}) fusion(f32[4,768,768]{2,1,0:T(8,128)} %get-tuple-element.26), kind=kLoop, calls=%fused_computation.8 | loop fusion | bytes 18874368 | tf_op jit(solution)/shard_map/squeeze | solution.py:1064
  337.7 19.9 %all-to-all-done.4 = bf16[8,2,96,384]{3,2,1,0:T(8,128)(2,1)S(1)} async-done(((bf16[8,2,96,384]{3,2,1,0:T(8,128)(2,1)}), bf16[8,2,96,384]{3,2,1,0:T(8,128)(2,1)S(1)}, u32[]{:S(2)}, u32[]{:S(2)}) %all-to-all-start.4) | async-done | bytes 1179680 | tf_op jit(solution)/shard_map/all_to_all | solution.py:732
  (148 shorter events, 34.6 us)
Async XLA Ops:
  7.2 66.4 %copy-start = (bf16[768,8]{0,1:T(8,128)(2,1)S(1)}, bf16[768,8]{0,1:T(8,128)(2,1)}, u32[]{:S(2)}) copy-start(bf16[768,8]{0,1:T(8,128)(2,1)} %param.24) | copy-start | bytes 36868
  9.4 5.4 %copy-start.31 = (bf16[768]{0:T(1024)(128)(2,1)S(1)}, bf16[768]{0:T(1024)(128)(2,1)}, u32[]{:S(2)}) copy-start(bf16[768]{0:T(1024)(128)(2,1)} %param.17) | copy-start | bytes 4612
  9.4 24.6 %all-to-all-start = ((bf16[4,256,768]{2,1,0:T(8,128)(2,1)}), bf16[4,256,768]{2,1,0:T(8,128)(2,1)S(1)}, u32[]{:S(2)}, u32[]{:S(2)}) async-start(bf16[4,256,768]{2,1,0:T(8,128)(2,1)} %broadcast_in_dim.32), calls=%async_computation | async-start | bytes 3145728 | tf_op jit(solution)/shard_map/all_to_all | solution.py:732
  14.8 20.2 %copy-start.15 = (f32[768]{0:T(1024)}, f32[768]{0:T(1024)S(1)}, u32[]{:S(2)}) copy-start(f32[768]{0:T(1024)S(1)} %convert_element_type.158) | copy-start | bytes 9220
  23.0 5.0 %copy-start.39 = (s32[8]{0:T(128)S(1)}, s32[8]{0:T(128)}, u32[]{:S(2)}) copy-start(s32[8]{0:T(128)} %param.15) | copy-start | bytes 100
  23.0 6.2 %copy-start.12 = (s32[256,1]{0,1:T(1,128)S(1)}, s32[256,1]{0,1:T(1,128)}, u32[]{:S(2)}) copy-start(s32[256,1]{0,1:T(1,128)} %param.16) | copy-start | bytes 3076
  39.2 23.3 %copy-start.36 = (bf16[768]{0:T(1024)(128)(2,1)S(1)}, bf16[768]{0:T(1024)(128)(2,1)}, u32[]{:S(2)}) copy-start(bf16[768]{0:T(1024)(128)(2,1)} %param.23) | copy-start | bytes 4612
  39.2 23.3 %copy-start.40 = (u32[32]{0:T(128)S(1)}, u32[32]{0:T(128)}, u32[]{:S(2)}) copy-start(u32[32]{0:T(128)} %constant.110) | copy-start | bytes 388
  39.2 31.4 %copy-start.1 = (bf16[768,768]{1,0:T(8,128)(2,1)S(1)}, bf16[768,768]{1,0:T(8,128)(2,1)}, u32[]{:S(2)}) copy-start(bf16[768,768]{1,0:T(8,128)(2,1)} %w_output_ref.1) | copy-start | bytes 3538948
  58.8 11.0 %all-to-all-start.1 = ((bf16[4,256,192]{1,2,0:T(8,128)(2,1)}), bf16[4,256,192]{1,2,0:T(8,128)(2,1)S(1)}, u32[]{:S(2)}, u32[]{:S(2)}) async-start(bf16[4,256,192]{1,2,0:T(8,128)(2,1)} %copy.68), calls=%async_computation.1 | async-start | bytes 786432 | tf_op jit(solution)/shard_map/all_to_all | solution.py:732
  62.2 244.2 %all-gather.3.cloned.1.call-start = ((), (), s32[]{:S(2)}) async-start(), calls=%async_computation.5 | async-start | bytes 10616832 | tf_op jit(solution)/shard_map/all_gather | solution.py:1031
  70.5 3.4 copy-start.13
  70.5 3.4 copy-start.32
  70.5 3.5 copy-start.4
  70.5 3.5 copy-start.20
  73.9 19.4 %copy-start.17 = (f32[256]{0:T(256)}, f32[256]{0:T(256)S(1)}, u32[]{:S(2)}) copy-start(f32[256]{0:T(256)S(1)} %get-tuple-element.52) | copy-start | bytes 3076
  73.9 19.3 %copy-start.22 = (f32[256]{0:T(256)}, f32[256]{0:T(256)S(1)}, u32[]{:S(2)}) copy-start(f32[256]{0:T(256)S(1)} %fusion.30) | copy-start | bytes 3076
  73.9 19.3 %copy-start.24 = (f32[256]{0:T(256)}, f32[256]{0:T(256)S(1)}, u32[]{:S(2)}) copy-start(f32[256]{0:T(256)S(1)} %select_reduce_fusion) | copy-start | bytes 3076
  74.0 19.3 %copy-start.29 = (f32[256]{0:T(256)}, f32[256]{0:T(256)S(1)}, u32[]{:S(2)}) copy-start(f32[256]{0:T(256)S(1)} %broadcast_select_fusion.1) | copy-start | bytes 3076
  115.3 20.1 %all-to-all-start.3 = ((bf16[8,48,1536]{2,1,0:T(8,128)(2,1)}), bf16[8,48,1536]{2,1,0:T(8,128)(2,1)S(1)}, u32[]{:S(2)}, u32[]{:S(2)}) async-start(bf16[8,48,1536]{2,1,0:T(8,128)(2,1)} %bitcast.82), calls=%async_computation.3 | async-start | bytes 2359296 | tf_op jit(solution)/shard_map/all_to_all | solution.py:732
  129.8 4.0 %copy-start.28 = (f32[1,2,4,128]{3,2,1,0:T(4,128)S(1)}, f32[1,2,4,128]{3,2,1,0:T(4,128)}, u32[]{:S(2)}) copy-start(f32[1,2,4,128]{3,2,1,0:T(4,128)} %get-tuple-element.46) | copy-start | bytes 12292
  129.8 4.0 %copy-start.16 = (f32[768]{0:T(1024)S(1)}, f32[768]{0:T(1024)}, u32[]{:S(2)}) copy-start(f32[768]{0:T(1024)} %copy-done.15) | copy-start | bytes 9220
  324.6 3.7 %copy-start.19 = (f32[24,768]{1,0:T(8,128)S(1)}, f32[24,768]{1,0:T(8,128)}, u32[]{:S(2)}) copy-start(f32[24,768]{1,0:T(8,128)} %get-tuple-element.25) | copy-start | bytes 221188
  324.6 33.0 %all-to-all-start.4 = ((bf16[8,2,96,384]{3,2,1,0:T(8,128)(2,1)}), bf16[8,2,96,384]{3,2,1,0:T(8,128)(2,1)S(1)}, u32[]{:S(2)}, u32[]{:S(2)}) async-start(bf16[8,2,96,384]{3,2,1,0:T(8,128)(2,1)} %bitcast.73), calls=%async_computation.4 | async-start | bytes 2359296 | tf_op jit(solution)/shard_map/all_to_all | solution.py:732
  (22 other events, 27.7 us)
Sparse Core Ops, SparseCore 0:
  94.5 187.4 all-gather.2
